TPU v7x, 512 devices: a whole 4x8x8 slice. The times are simulated.
512 devices in a mesh: gx: 32 (over y, x), gy: 16 (over z, core).
Axes of the slice: x: 4, y: 8, z: 8, core: 2. Of those that a mesh axis runs over, the one named last changes fastest.
Arguments:
- basis: float32 [22, 6, 20, 65536], P(None, None, None, ('gx', 'gy'))
- geometry: float32 [9, 65536], P(None, ('gx', 'gy')), may hold values from -0.3 to 0.3
- face_normals: float32 [3, 4, 65536], P(None, None, ('gx', 'gy')), may hold values from -3 to 3
- face_scale: float32 [4, 65536], P(None, ('gx', 'gy')), may hold values from 0.02 to 0.2
- material: float32 [3, 65536], P(None, ('gx', 'gy')), may hold values from 0.25 to 4
- send_list: int32 [96, 48, 64], P('gx', 'gy'), may hold values from 0 to 511, as said below
- neighbour_source: int32 [4, 65536], P(None, ('gx', 'gy')), may hold values from 0 to 1087, as said below
- node_rotation: int32 [4, 65536], P(None, ('gx', 'gy')), may hold values from 0 to 2
- boundary_flag: int32 [4, 65536], P(None, ('gx', 'gy')), may hold values from 0 to 1
Outputs:
- new_basis: float32 [2, 6, 20, 65536], P(None, None, None, ('gx', 'gy'))
- hessenberg: float32 [2, 24], replicated
Inputs may be any that keep to these rules, and one draw needn't show every extreme that they name: `send_list`: block (a, b) of device (i, j) lists local face ids meant for device (i + a - 1, j + b - 1); only the slots that device reads carry meaning; block (1, 1) is never read. `basis`: the stored vectors need not be orthonormal or of unit norm under <u, w>; the steps hold as written for any stored vectors. `neighbour_source`: remote sources always name an existing device. Faces pair up across devices: a device reads from one neighbour slots 0 to c - 1 of its block, with c at most 64, and c reaches 64 for some pairs in every draw. Faces with boundary_flag 1 ignore their source.
All inputs are finite; a program needn't handle non-finite values.
Results may differ from a plain program's by a relative error of at most 0.0003.
Values sent between devices are 32-bit elements; how exact they have to be, the bound alone decides.
A program may use at most 64 MiB of HBM per device.

v0:
```python
import math

import jax
import jax.numpy as jnp
import numpy as np
from jax import lax
from jax.sharding import PartitionSpec as P

highest = lax.Precision.HIGHEST


def padded_2(block, sides, width):
    for axis, dim in sides:
        count = lax.axis_size(axis)
        forward = [(i, i + 1) for i in range(count - 1)]
        backward = [(target, source) for source, target in forward]
        low = lax.ppermute(
            lax.slice_in_dim(block, block.shape[dim] - width, None, axis=dim), axis, forward
        )
        high = lax.ppermute(lax.slice_in_dim(block, 0, width, axis=dim), axis, backward)
        block = jnp.concatenate([low, block, high], axis=dim)
    return block


def invert(matrix):
    dimension = len(matrix)
    augmented = []
    for row_index in range(dimension):
        augmented.append(
            [float(matrix[row_index][column]) for column in range(dimension)]
            + [1.0 if column == row_index else 0.0 for column in range(dimension)]
        )
    for column in range(dimension):
        pivot_row = column
        for row_index in range(column + 1, dimension):
            if abs(augmented[row_index][column]) > abs(augmented[pivot_row][column]):
                pivot_row = row_index
        augmented[column], augmented[pivot_row] = (augmented[pivot_row], augmented[column])
        leading = augmented[column][column]
        augmented[column] = [value / leading for value in augmented[column]]
        for row_index in range(dimension):
            if row_index != column:
                factor = augmented[row_index][column]
                augmented[row_index] = [
                    left - factor * right
                    for left, right in zip(augmented[row_index], augmented[column])
                ]
    return np.array([entries[dimension:] for entries in augmented])


def locate(face, first, second):
    if face == 0:
        return (first, second, 0)
    if face == 1:
        return (first, 0, second)
    if face == 2:
        return (3 - first - second, first, second)
    return (0, first, second)


def element_tables():
    nodes = [(i, j, k) for k in range(4) for j in range(4) for i in range(4) if i + j + k <= 3]
    points = np.array(nodes) / 3.0
    vander = np.zeros((20, 20))
    slopes = np.zeros((3, 20, 20))
    for row in range(20):
        for column in range(20):
            powers = np.array(nodes[column])
            vander[row, column] = np.prod(points[row] ** powers)
            for axis in range(3):
                if powers[axis] > 0:
                    lowered = powers.copy()
                    lowered[axis] -= 1
                    slopes[axis, row, column] = powers[axis] * np.prod(points[row] ** lowered)
    inverse = invert(vander)
    derivs = np.stack([slopes[axis] @ inverse for axis in range(3)])
    moments = np.zeros((20, 20))
    for row in range(20):
        for column in range(20):
            left = nodes[row]
            right = nodes[column]
            sums = [left[0] + right[0], left[1] + right[1], left[2] + right[2]]
            moments[row, column] = (
                math.factorial(sums[0])
                * math.factorial(sums[1])
                * math.factorial(sums[2])
                / math.factorial(sum(sums) + 3)
            )
    mass = inverse.T @ moments @ inverse
    lattice = [(first, second) for second in range(4) for first in range(4) if first + second <= 3]
    face_nodes = np.array(
        [[nodes.index(locate(face, pair[0], pair[1])) for face in range(4)] for pair in lattice]
    )
    plane = np.array(
        [
            [(pair[0] / 3.0) ** expo[0] * (pair[1] / 3.0) ** expo[1] for expo in lattice]
            for pair in lattice
        ]
    )
    plane_inverse = invert(plane)
    plane_moments = np.zeros((10, 10))
    for row in range(10):
        for column in range(10):
            first = lattice[row][0] + lattice[column][0]
            second = lattice[row][1] + lattice[column][1]
            plane_moments[row, column] = (
                math.factorial(first) * math.factorial(second) / math.factorial(first + second + 2)
            )
    face_mass = plane_inverse.T @ plane_moments @ plane_inverse
    edges = np.zeros((20, 40))
    for face in range(4):
        for row in range(10):
            for column in range(10):
                edges[face_nodes[row, face], column * 4 + face] += face_mass[row, column]
    lift = invert(mass) @ edges
    turned = np.array([lattice.index((pair[1], 3 - pair[0] - pair[1])) for pair in lattice])
    rotations = np.stack([np.arange(10), turned, turned[turned]])
    return (derivs, lift, face_nodes, rotations)


def curl_pair(field, geometry, derivs):
    along = jnp.einsum("qnm,cme->qcne", derivs, field, precision=highest)
    grads = [
        along[0] * geometry[axis] + along[1] * geometry[3 + axis] + along[2] * geometry[6 + axis]
        for axis in range(3)
    ]
    curl_e = jnp.stack(
        [grads[1][2] - grads[2][1], grads[2][0] - grads[0][2], grads[0][1] - grads[1][0]]
    )
    curl_h = jnp.stack(
        [grads[1][5] - grads[2][4], grads[2][3] - grads[0][5], grads[0][4] - grads[1][3]]
    )
    return (curl_e, curl_h)


def turn_nodes(other, turns, rotations):
    first = other[:, rotations[1], :]
    second = other[:, rotations[2], :]
    return jnp.where(turns == 0, other, jnp.where(turns == 1, first, second))


def flux_terms(inside, other, flags, normals, scale):
    wall = flags == 1
    other_e = jnp.where(wall, -inside[:3], other[:3])
    other_h = jnp.where(wall, inside[3:], other[3:])
    jump_e = other_e - inside[:3]
    jump_h = other_h - inside[3:]
    normal_x = normals[0]
    normal_y = normals[1]
    normal_z = normals[2]
    along_e = normal_x * jump_e[0] + normal_y * jump_e[1] + normal_z * jump_e[2]
    along_h = normal_x * jump_h[0] + normal_y * jump_h[1] + normal_z * jump_h[2]
    flux = jnp.stack(
        [
            normal_y * jump_h[2] - normal_z * jump_h[1] + jump_e[0] - along_e * normal_x,
            normal_z * jump_h[0] - normal_x * jump_h[2] + jump_e[1] - along_e * normal_y,
            normal_x * jump_h[1] - normal_y * jump_h[0] + jump_e[2] - along_e * normal_z,
            -normal_y * jump_e[2] + normal_z * jump_e[1] + jump_h[0] - along_h * normal_x,
            -normal_z * jump_e[0] + normal_x * jump_e[2] + jump_h[1] - along_h * normal_y,
            -normal_x * jump_e[1] + normal_y * jump_e[0] + jump_h[2] - along_h * normal_z,
        ]
    )
    return flux * (0.5 * scale)


def assemble(field, curl_e, curl_h, flux, lift, material):
    count = field.shape[2]
    lifted = jnp.einsum("nk,cke->cne", lift, flux.reshape(6, 40, count), precision=highest)
    electric = material[0] * (curl_h + lifted[:3]) - material[2] * field[:3]
    magnetic = material[1] * (lifted[3:] - curl_e)
    return jnp.concatenate([electric, magnetic], axis=0)


def body(
    basis,
    geometry,
    face_normals,
    face_scale,
    material,
    send_list,
    neighbour_source,
    node_rotation,
    boundary_flag,
):
    derivs_np, lift_np, face_nodes, rotations = element_tables()
    derivs = jnp.asarray(derivs_np, dtype=jnp.float32)
    lift = jnp.asarray(lift_np, dtype=jnp.float32)
    kept = basis.shape[0]
    components = basis.shape[1]
    nodes = basis.shape[2]
    local_count = basis.shape[3]
    faces_here = 4 * local_count
    slot_width = send_list.shape[2]
    total = float(components * nodes * local_count * lax.axis_size("gx") * lax.axis_size("gy"))
    normals = face_normals.reshape(3, faces_here)
    scale = face_scale.reshape(-1)
    flags = boundary_flag.reshape(-1)
    turns = node_rotation.reshape(-1)
    outgoing_index = send_list.reshape(-1)
    source = neighbour_source.reshape(-1)
    stacked = basis.reshape(kept, -1)
    fresh = jnp.zeros((2, stacked.shape[1]), jnp.float32)
    current = stacked[kept - 1]
    columns = []
    for turn in range(2):
        field = current.reshape(components, nodes, local_count)
        curl_e, curl_h = curl_pair(field, geometry, derivs)
        inside = field[:, face_nodes, :].reshape(60, faces_here)
        outgoing = jnp.take(inside, outgoing_index, axis=1)
        padded = padded_2(outgoing.reshape(60, 3, 3, slot_width), (("gx", 1), ("gy", 2)), 1)
        arrived = padded[:, 0::2, 0::2, :].reshape(60, 9 * slot_width)
        table = jnp.concatenate([inside, arrived], axis=1)
        other = jnp.take(table, source, axis=1).reshape(6, 10, faces_here)
        other = turn_nodes(other, turns, rotations)
        flux = flux_terms(inside.reshape(6, 10, faces_here), other, flags, normals, scale)
        image = assemble(field, curl_e, curl_h, flux, lift, material).reshape(-1)
        part_v = jnp.dot(stacked, image, precision=highest)
        part_n = jnp.dot(fresh, image, precision=highest)
        first_v, first_n = lax.psum((part_v, part_n), ("gx", "gy"))
        first_v = first_v / total
        first_n = first_n / total
        image = (
            image
            - jnp.dot(first_v, stacked, precision=highest)
            - jnp.dot(first_n, fresh, precision=highest)
        )
        part_v = jnp.dot(stacked, image, precision=highest)
        part_n = jnp.dot(fresh, image, precision=highest)
        second_v, second_n = lax.psum((part_v, part_n), ("gx", "gy"))
        second_v = second_v / total
        second_n = second_n / total
        image = (
            image
            - jnp.dot(second_v, stacked, precision=highest)
            - jnp.dot(second_n, fresh, precision=highest)
        )
        square = lax.psum(jnp.sum(image * image), ("gx", "gy")) / total
        height = jnp.sqrt(square + 1e-06)
        current = image / height
        fresh = fresh.at[turn].set(current)
        column = (
            jnp.concatenate([first_v + second_v, first_n + second_n]).at[kept + turn].set(height)
        )
        columns.append(column)
    return (fresh.reshape(2, components, nodes, local_count), jnp.stack(columns))


def solution(mesh):
    placed = (
        P(None, None, None, ("gx", "gy")),
        P(None, ("gx", "gy")),
        P(None, None, ("gx", "gy")),
        P(None, ("gx", "gy")),
        P(None, ("gx", "gy")),
        P("gx", "gy", None),
        P(None, ("gx", "gy")),
        P(None, ("gx", "gy")),
        P(None, ("gx", "gy")),
    )
    return jax.shard_map(
        body,
        mesh=mesh,
        in_specs=placed,
        out_specs=(P(None, None, None, ("gx", "gy")), P()),
        check_vma=False,
    )
```

profile of v0, /device:TPU:1, one launch (start us, length us, event | category | flops | bytes accessed | tf_op | source)
XLA Modules:
  0.0 688.3 jit_solution(16794183504935588408)
XLA Ops:
  0.6 0.8 reshape.679
  1.4 1.7 copy.68
  4.8 1.6 gather_fusion.6
  6.6 0.7 fusion.79
  7.3 1.3 collective-permute-start.1
  8.6 4.6 collective-permute-start
  19.4 1.5 slice.426
  20.9 1.5 slice.415
  22.4 1.0 pad_maximum_fusion.9
  23.4 8.8 %collective-permute-start.3 = (f32[60,5,1,64]{0,3,2,1:T(8,128)S(1)}, f32[60,5,1,64]{0,3,2,1:T(8,128)S(1)}, u32[]{:S(2)}, u32[]{:S(2)}) collective-permute-start(f32[60,5,1,64]{0,3,2,1:T(8,128)S(1)} %get-tuple-element.71), channel_id=1, source_target_pairs={{1,0},{2,1},{3,2},{4,3},{5,4},{6,5},{7,6},{8,7},{9,8},{10,9},{11,1... | collective-permute-start | bytes 230408 | tf_op jit(solution)/shard_map/ppermute | solution.py:20
  32.2 1.9 collective-permute-start.2
  34.1 0.7 pad_clamp_fusion
  34.8 1.5 collective-permute-done.2
  36.3 1.0 pad_maximum_fusion
  37.5 1.0 gather_fusion.7
  40.1 0.9 bitcast_select_fusion.1
  41.0 0.9 fusion.9
  41.9 0.8 multiply_subtract_fusion.6
  42.8 0.9 multiply_subtract_fusion.7
  43.7 0.7 mul.667
  44.4 0.9 convolution_bitcast_fusion.3
  45.4 0.9 fusion.27
  46.3 1.1 convolution_bitcast_fusion.11
  47.4 1.5 convolution_bitcast_fusion.7
  49.0 102.6 %all-reduce.4 = (f32[2]{0:T(128)S(1)}, f32[22]{0:T(128)S(1)}) all-reduce(f32[2]{0:T(128)S(1)} %convolution_bitcast_fusion.11, f32[22]{0:T(128)S(1)} %convolution_bitcast_fusion.7), channel_id=1, replica_groups=mesh['gx'=32,'gy'=16] {'gx','gy'}, use_global_device_ids=true, to_apply=%region_1.4 | all-reduce | flops 24 | bytes 192 | tf_op jit(solution)/shard_map/psum | solution.py:219
  152.1 0.9 fusion.35
  153.0 1.5 convolution_bitcast_fusion.6
  154.4 1.1 convolution_bitcast_fusion.10
  155.6 94.5 %all-reduce.3 = (f32[2]{0:T(128)S(1)}, f32[22]{0:T(128)S(1)}) all-reduce(f32[2]{0:T(128)S(1)} %convolution_bitcast_fusion.10, f32[22]{0:T(128)S(1)} %convolution_bitcast_fusion.6), channel_id=1, replica_groups=mesh['gx'=32,'gy'=16] {'gx','gy'}, use_global_device_ids=true, to_apply=%region_3.6 | all-reduce | flops 24 | bytes 192 | tf_op jit(solution)/shard_map/psum | solution.py:229
  250.7 0.9 fusion.33
  252.2 94.4 %psum.74 = f32[]{:T(128)} all-reduce(f32[]{:T(128)} %multiply_reduce_fusion.1), channel_id=1, replica_groups=mesh['gx'=32,'gy'=16] {'gx','gy'}, use_global_device_ids=true, to_apply=%region_5.8 | all-reduce | flops 1 | bytes 8 | tf_op jit(solution)/shard_map/psum | solution.py:237
  350.1 2.2 gather_fusion.8
  352.4 1.1 broadcast_select_fusion
  353.5 0.7 fusion.78
  354.2 1.3 collective-permute-start.5
  355.5 4.6 collective-permute-start.4
  360.2 1.2 convolution_bitcast_fusion
  361.4 0.7 multiply_add_fusion.1
  363.4 1.5 slice.465
  364.9 1.5 copy.83
  366.4 1.5 slice.455
  368.5 0.8 pad_maximum_fusion.6
  369.4 3.1 collective-permute-start.7
  372.5 3.2 collective-permute-start.6
  376.8 1.2 collective-permute-done.6
  377.9 1.0 pad_maximum_fusion.1
  379.0 0.9 pad_maximum_fusion.3
  379.9 2.1 gather_fusion.9
  382.0 0.8 select_bitcast_fusion
  383.7 1.3 gather_fusion.5
  385.1 1.1 bitcast_select_fusion
  386.2 0.9 fusion.8
  387.2 0.8 multiply_subtract_fusion
  388.0 0.9 multiply_subtract_fusion.1
  389.4 1.5 convolution_bitcast_fusion.5
  390.9 1.2 convolution_bitcast_fusion.9
  392.1 97.5 %all-reduce.2 = (f32[2]{0:T(128)S(1)}, f32[22]{0:T(128)S(1)}) all-reduce(f32[2]{0:T(128)S(1)} %convolution_bitcast_fusion.9, f32[22]{0:T(128)S(1)} %convolution_bitcast_fusion.5), channel_id=1, replica_groups=mesh['gx'=32,'gy'=16] {'gx','gy'}, use_global_device_ids=true, to_apply=%region_7.10 | all-reduce | flops 24 | bytes 192 | tf_op jit(solution)/shard_map/psum | solution.py:219
  490.2 0.9 fusion.31
  491.1 1.2 convolution_bitcast_fusion.8
  492.3 1.5 convolution_bitcast_fusion.4
  493.9 94.8 %all-reduce.1 = (f32[2]{0:T(128)S(1)}, f32[22]{0:T(128)S(1)}) all-reduce(f32[2]{0:T(128)S(1)} %convolution_bitcast_fusion.8, f32[22]{0:T(128)S(1)} %convolution_bitcast_fusion.4), channel_id=1, replica_groups=mesh['gx'=32,'gy'=16] {'gx','gy'}, use_global_device_ids=true, to_apply=%region_9.12 | all-reduce | flops 24 | bytes 192 | tf_op jit(solution)/shard_map/psum | solution.py:229
  589.3 0.9 fusion.29
  590.8 95.3 %psum.79 = f32[]{:T(128)} all-reduce(f32[]{:T(128)} %multiply_reduce_fusion), channel_id=1, replica_groups=mesh['gx'=32,'gy'=16] {'gx','gy'}, use_global_device_ids=true, to_apply=%region_11.14 | all-reduce | flops 1 | bytes 8 | tf_op jit(solution)/shard_map/psum | solution.py:237
  686.7 0.8 pad_maximum_fusion.10
  (218 shorter events, 20.7 us)
Async XLA Ops:
  1.4 5.0 copy-start.26
  1.4 1.7 copy-start.56
  3.1 16.1 %copy-start.1 = (f32[22,6,20,128]{3,2,1,0:T(8,128)}, f32[22,6,20,128]{3,2,1,0:T(8,128)S(1)}, u32[]{:S(2)}) copy-start(f32[22,6,20,128]{3,2,1,0:T(8,128)S(1)} %copy.68) | copy-start | bytes 4055044
  4.0 9.2 %copy-start.23 = (f32[3,4,128]{2,1,0:T(4,128)S(1)}, f32[3,4,128]{2,1,0:T(4,128)}, u32[]{:S(2)}) copy-start(f32[3,4,128]{2,1,0:T(4,128)} %param.36) | copy-start | bytes 18436
  4.7 10.9 %copy-start.21 = (s32[1024]{0:T(1024)}, s32[1024]{0:T(1024)S(1)}, u32[]{:S(2)}) copy-start(s32[1024]{0:T(1024)S(1)} %get-tuple-element.157) | copy-start | bytes 12292
  4.7 10.9 %copy-start.49 = (s32[4,128]{1,0:T(4,128)S(1)}, s32[4,128]{1,0:T(4,128)}, u32[]{:S(2)}) copy-start(s32[4,128]{1,0:T(4,128)} %param.41) | copy-start | bytes 6148
  4.7 11.5 %copy-start.50 = (f32[4,128]{1,0:T(4,128)S(1)}, f32[4,128]{1,0:T(4,128)}, u32[]{:S(2)}) copy-start(f32[4,128]{1,0:T(4,128)} %param.37) | copy-start | bytes 6148
  4.7 12.1 %copy-start.11 = (f32[3,20,20,1]{2,1,3,0:T(8,128)S(1)}, f32[3,20,20,1]{2,1,3,0:T(8,128)}, u32[]{:S(2)}) copy-start(f32[3,20,20,1]{2,1,3,0:T(8,128)} %constant.190) | copy-start | bytes 14404
  4.7 12.4 %copy-start.47 = (f32[9,128]{1,0:T(8,128)S(1)}, f32[9,128]{1,0:T(8,128)}, u32[]{:S(2)}) copy-start(f32[9,128]{1,0:T(8,128)} %param.35) | copy-start | bytes 13828
  4.7 12.4 %copy-start.51 = (f32[3,128]{1,0:T(4,128)S(1)}, f32[3,128]{1,0:T(4,128)}, u32[]{:S(2)}) copy-start(f32[3,128]{1,0:T(4,128)} %param.38) | copy-start | bytes 4612
  6.4 12.2 %copy-start.48 = (s32[4,128]{1,0:T(4,128)S(1)}, s32[4,128]{1,0:T(4,128)}, u32[]{:S(2)}) copy-start(s32[4,128]{1,0:T(4,128)} %param.42) | copy-start | bytes 6148
  6.6 12.0 %copy-start.2 = (f32[576,60]{1,0:T(8,128)}, f32[576,60]{1,0:T(8,128)S(1)}, u32[]{:S(2)}) copy-start(f32[576,60]{1,0:T(8,128)S(1)} %broadcast_select_fusion.1) | copy-start | bytes 414724
  7.3 15.1 %collective-permute-start.1 = (f32[60,1,3,64]{0,3,2,1:T(8,128)}, f32[60,1,3,64]{0,3,2,1:T(8,128)S(1)}, u32[]{:S(2)}, u32[]{:S(2)}) collective-permute-start(f32[60,1,3,64]{0,3,2,1:T(8,128)} %get-tuple-element.75), channel_id=1, source_target_pairs={{16,0},{32,16},{48,32},{64,48},{80,64},{96,80},{112,96},{128,112},... | collective-permute-start | bytes 138248 | tf_op jit(solution)/shard_map/ppermute | solution.py:20
  8.6 13.8 %collective-permute-start = (f32[60,1,3,64]{0,3,2,1:T(8,128)}, f32[60,1,3,64]{0,3,2,1:T(8,128)S(1)}, u32[]{:S(2)}, u32[]{:S(2)}) collective-permute-start(f32[60,1,3,64]{0,3,2,1:T(8,128)} %get-tuple-element.74), channel_id=1, source_target_pairs={{0,16},{16,32},{32,48},{48,64},{64,80},{80,96},{96,112},{112,128},... | collective-permute-start | bytes 138248 | tf_op jit(solution)/shard_map/ppermute | solution.py:17
  17.2 1.4 copy-start.35
  17.2 1.4 copy-start.37
  17.2 1.4 copy-start.39
  17.2 1.4 copy-start.41
  17.2 1.4 copy-start.42
  17.2 1.4 copy-start.43
  17.2 1.4 copy-start.44
  17.3 1.4 copy-start.45
  23.4 11.4 %collective-permute-start.3 = (f32[60,5,1,64]{0,3,2,1:T(8,128)S(1)}, f32[60,5,1,64]{0,3,2,1:T(8,128)S(1)}, u32[]{:S(2)}, u32[]{:S(2)}) collective-permute-start(f32[60,5,1,64]{0,3,2,1:T(8,128)S(1)} %get-tuple-element.71), channel_id=1, source_target_pairs={{1,0},{2,1},{3,2},{4,3},{5,4},{6,5},{7,6},{8,7},{9,8},{10,9},{11,1... | collective-permute-start | bytes 230408 | tf_op jit(solution)/shard_map/ppermute | solution.py:20
  32.2 4.2 collective-permute-start.2
  34.8 4.2 copy-start.30
  34.8 4.7 copy-start.29
  34.8 2.7 copy-start.24
  38.5 2.5 copy-start.6
  40.1 7.4 %copy-start = (f32[22,6,20,128]{3,0,2,1:T(8,128)S(1)}, f32[22,6,20,128]{3,0,2,1:T(8,128)}, u32[]{:S(2)}) copy-start(f32[22,6,20,128]{3,0,2,1:T(8,128)} %param.34) | copy-start | bytes 4055044
  44.4 1.8 copy-start.8
  151.5 1.4 copy-start.52
  154.4 192.9 %copy-start.13 = (s32[1024]{0:T(1024)S(1)}, s32[1024]{0:T(1024)}, u32[]{:S(2)}) copy-start(s32[1024]{0:T(1024)} %copy-done.12) | copy-start | bytes 12292
  250.1 97.1 %copy-start.54 = (f32[22]{0:T(128)}, f32[22]{0:T(128)S(1)}, u32[]{:S(2)}) copy-start(f32[22]{0:T(128)S(1)} %get-tuple-element.57) | copy-start | bytes 268
  251.5 98.5 %copy-start.22 = (s32[1024]{0:T(1024)S(1)}, s32[1024]{0:T(1024)}, u32[]{:S(2)}) copy-start(s32[1024]{0:T(1024)} %copy-done.21) | copy-start | bytes 12292
  347.3 2.6 copy-start.3
  348.0 4.3 copy-start.27
  350.1 11.3 %copy-start.36 = (f32[128]{0:T(128)S(1)}, f32[128]{0:T(128)}, u32[]{:S(2)}) copy-start(f32[128]{0:T(128)} %copy-done.35) | copy-start | bytes 1540
  350.1 11.3 %copy-start.38 = (f32[128]{0:T(128)S(1)}, f32[128]{0:T(128)}, u32[]{:S(2)}) copy-start(f32[128]{0:T(128)} %copy-done.37) | copy-start | bytes 1540
  350.1 11.3 %copy-start.40 = (f32[128]{0:T(128)S(1)}, f32[128]{0:T(128)}, u32[]{:S(2)}) copy-start(f32[128]{0:T(128)} %copy-done.39) | copy-start | bytes 1540
  352.4 10.4 %copy-start.53 = (f32[22]{0:T(128)S(1)}, f32[22]{0:T(128)}, u32[]{:S(2)}) copy-start(f32[22]{0:T(128)} %copy-done.52) | copy-start | bytes 268
  352.4 10.4 %copy-start.55 = (f32[22]{0:T(128)S(1)}, f32[22]{0:T(128)}, u32[]{:S(2)}) copy-start(f32[22]{0:T(128)} %copy-done.54) | copy-start | bytes 268
  352.4 10.4 %copy-start.7 = (f32[3,10,4,128]{3,2,1,0:T(4,128)S(1)}, f32[3,10,4,128]{3,2,1,0:T(4,128)}, u32[]{:S(2)}) copy-start(f32[3,10,4,128]{3,2,1,0:T(4,128)} %get-tuple-element.114) | copy-start | bytes 184324
  352.4 15.5 %slice-start = ((f32[15360]{0:T(1024)}), f32[7680]{0:T(1024)S(1)}, s32[]{:S(2)}) async-start(f32[15360]{0:T(1024)} %copy-done.3), calls=%async_computation | async-start | bytes 65536 | tf_op jit(solution)/shard_map/slice | solution.py:169
  353.5 22.2 %copy-start.58 = (f32[2]{0:T(128)S(1)}, f32[2]{0:T(128)}, u32[]{:S(2)}) copy-start(f32[2]{0:T(128)} %multiply_add_fusion.12) | copy-start | bytes 28
  354.2 14.3 %collective-permute-start.5 = (f32[60,1,3,64]{0,3,2,1:T(8,128)}, f32[60,1,3,64]{0,3,2,1:T(8,128)}, u32[]{:S(2)}, u32[]{:S(2)}) collective-permute-start(f32[60,1,3,64]{0,3,2,1:T(8,128)} %get-tuple-element.73), channel_id=1, source_target_pairs={{16,0},{32,16},{48,32},{64,48},{80,64},{96,80},{112,96},{128,112},... | collective-permute-start | bytes 138248 | tf_op jit(solution)/shard_map/ppermute | solution.py:20
  355.5 13.0 %collective-permute-start.4 = (f32[60,1,3,64]{0,3,2,1:T(8,128)}, f32[60,1,3,64]{0,3,2,1:T(8,128)}, u32[]{:S(2)}, u32[]{:S(2)}) collective-permute-start(f32[60,1,3,64]{0,3,2,1:T(8,128)} %get-tuple-element.72), channel_id=1, source_target_pairs={{0,16},{16,32},{32,48},{48,64},{64,80},{80,96},{96,112},{112,128},... | collective-permute-start | bytes 138248 | tf_op jit(solution)/shard_map/ppermute | solution.py:17
  369.4 7.4 %collective-permute-start.7 = (f32[60,5,1,64]{0,3,2,1:T(8,128)S(1)}, f32[60,5,1,64]{0,3,2,1:T(8,128)S(1)}, u32[]{:S(2)}, u32[]{:S(2)}) collective-permute-start(f32[60,5,1,64]{0,3,2,1:T(8,128)S(1)} %get-tuple-element.69), channel_id=1, source_target_pairs={{1,0},{2,1},{3,2},{4,3},{5,4},{6,5},{7,6},{8,7},{9,8},{10,9},{11,1... | collective-permute-start | bytes 230408 | tf_op jit(solution)/shard_map/ppermute | solution.py:20
  372.5 5.4 collective-permute-start.6
  376.3 3.6 copy-start.25
  382.0 4.2 copy-start.5
  385.0 4.0 copy-start.9
  385.0 4.0 copy-start.14
  385.0 4.2 copy-start.10
  385.0 4.2 copy-start.15
  385.0 4.2 copy-start.16
  385.0 4.2 copy-start.17
  385.1 4.2 copy-start.18
  385.1 4.2 copy-start.19
  385.1 4.2 copy-start.20
  385.1 4.2 copy-start.32
  385.1 4.2 copy-start.33
  385.1 4.2 copy-start.34
  388.0 2.9 copy-start.4
  490.2 3.6 copy-start.57
  (4 other events, 4.2 us)
where the time goes:
time: 690 us; the launch traced here: 688 us
  blocking collectives  579 us (84%)
  local copies, waits for them, and re-layouts  29.7 us (4%)
  starting transfers between devices  28.8 us (4%)
  other arithmetic  25.2 us (4%)
  matrix products  18.8 us (3%)
    psum x2, blocking collectives, body(): first_v, first_n = lax.psum((part_v, part_n), ('gx', 'gy'))  200 us
    psum x2, blocking collectives, body(): square = lax.psum(jnp.sum(image * image), ('gx', 'gy')) / total  190 us
    psum x2, blocking collectives, body(): second_v, second_n = lax.psum((part_v, part_n), ('gx', 'gy'))  189 us
    ppermute x4, starting transfers between devices, padded_2(): lax.ppermute(lax.slice_in_dim(block, 0, width, axis=dim), axis, backward)  14.4 us
    ppermute x4, starting transfers between devices, padded_2(): lax.ppermute(lax.slice_in_dim(block, block.shape[dim] - width, None, axis...  14.3 us
  transfers between devices with their start and end apart: 8, of which 3 were waited for; matrix products, arithmetic and copies ran while one was open for 3% of the time, Pallas kernels for 0%

commit v1 on v0

v1 whole, which is shorter than its diff:
```python
import functools
import math

import jax
import jax.numpy as jnp
import numpy as np
from jax import lax
from jax.experimental import pallas as pl
from jax.experimental.pallas import tpu as pltpu
from jax.sharding import PartitionSpec as P

MESH = pl.DeviceIdType.MESH
X_CHIPS = 4
OPERANDS = (0, 64, 144, 176)
DIRECTIONS = (0, 1, 2, 3, 5, 6, 7, 8)


def invert(matrix):
    dimension = len(matrix)
    augmented = []
    for row_index in range(dimension):
        augmented.append(
            [float(matrix[row_index][column]) for column in range(dimension)]
            + [1.0 if column == row_index else 0.0 for column in range(dimension)]
        )
    for column in range(dimension):
        pivot_row = column
        for row_index in range(column + 1, dimension):
            if abs(augmented[row_index][column]) > abs(augmented[pivot_row][column]):
                pivot_row = row_index
        augmented[column], augmented[pivot_row] = (augmented[pivot_row], augmented[column])
        leading = augmented[column][column]
        augmented[column] = [value / leading for value in augmented[column]]
        for row_index in range(dimension):
            if row_index != column:
                factor = augmented[row_index][column]
                augmented[row_index] = [
                    left - factor * right
                    for left, right in zip(augmented[row_index], augmented[column])
                ]
    return np.array([entries[dimension:] for entries in augmented])


def locate(face, first, second):
    if face == 0:
        return (first, second, 0)
    if face == 1:
        return (first, 0, second)
    if face == 2:
        return (3 - first - second, first, second)
    return (0, first, second)


def element_tables():
    nodes = [(i, j, k) for k in range(4) for j in range(4) for i in range(4) if i + j + k <= 3]
    points = np.array(nodes) / 3.0
    vander = np.zeros((20, 20))
    slopes = np.zeros((3, 20, 20))
    for row in range(20):
        for column in range(20):
            powers = np.array(nodes[column])
            vander[row, column] = np.prod(points[row] ** powers)
            for axis in range(3):
                if powers[axis] > 0:
                    lowered = powers.copy()
                    lowered[axis] -= 1
                    slopes[axis, row, column] = powers[axis] * np.prod(points[row] ** lowered)
    inverse = invert(vander)
    derivs = np.stack([slopes[axis] @ inverse for axis in range(3)])
    moments = np.zeros((20, 20))
    for row in range(20):
        for column in range(20):
            left = nodes[row]
            right = nodes[column]
            sums = [left[0] + right[0], left[1] + right[1], left[2] + right[2]]
            moments[row, column] = (
                math.factorial(sums[0])
                * math.factorial(sums[1])
                * math.factorial(sums[2])
                / math.factorial(sum(sums) + 3)
            )
    mass = inverse.T @ moments @ inverse
    lattice = [(first, second) for second in range(4) for first in range(4) if first + second <= 3]
    face_nodes = np.array(
        [[nodes.index(locate(face, pair[0], pair[1])) for face in range(4)] for pair in lattice]
    )
    plane = np.array(
        [
            [(pair[0] / 3.0) ** expo[0] * (pair[1] / 3.0) ** expo[1] for expo in lattice]
            for pair in lattice
        ]
    )
    plane_inverse = invert(plane)
    plane_moments = np.zeros((10, 10))
    for row in range(10):
        for column in range(10):
            first = lattice[row][0] + lattice[column][0]
            second = lattice[row][1] + lattice[column][1]
            plane_moments[row, column] = (
                math.factorial(first) * math.factorial(second) / math.factorial(first + second + 2)
            )
    face_mass = plane_inverse.T @ plane_moments @ plane_inverse
    edges = np.zeros((20, 40))
    for face in range(4):
        for row in range(10):
            for column in range(10):
                edges[face_nodes[row, face], column * 4 + face] += face_mass[row, column]
    lift = invert(mass) @ edges
    turned = np.array([lattice.index((pair[1], 3 - pair[0] - pair[1])) for pair in lattice])
    rotations = np.stack([np.arange(10), turned, turned[turned]])
    return (derivs, lift, face_nodes, rotations)


def bf16_parts(values):
    values = np.asarray(values, np.float32)
    high = values.astype(jnp.bfloat16)
    rest = values - high.astype(np.float32)
    middle = rest.astype(jnp.bfloat16)
    low = (rest - middle.astype(np.float32)).astype(jnp.bfloat16)
    return high, middle, low


def packed_row(component, node):
    return 8 * component + node if node < 8 else 48 + 2 * component + node - 8


def left_operands():
    derivs, lift, face_nodes, rotations = element_tables()
    pick = np.zeros((64, 32), np.float32)
    for face in range(4):
        for node in range(10):
            pick[16 * face + node, face_nodes[node, face]] = 1.0
    traces = np.concatenate([pick, pick, pick], axis=1)
    stack = np.zeros((3, 80, 32), np.float32)
    for index, part in enumerate(bf16_parts(derivs)):
        for axis in range(3):
            stack[index, 24 * axis : 24 * axis + 20, :20] = part[axis].astype(np.float32)
    high, middle, low = stack
    volume = np.concatenate([high, high, high, middle, low, middle], axis=1)
    blocks = np.zeros((3, 32, 64), np.float32)
    for index, part in enumerate(bf16_parts(lift)):
        for face in range(4):
            for node in range(10):
                blocks[index, :20, 16 * face + node] = part[:, node * 4 + face].astype(np.float32)
    raise_up = np.concatenate([blocks[0], blocks[1], blocks[0], blocks[0]], axis=1)
    spread = np.zeros((288, 64), np.float32)
    for turn in range(3):
        for component in range(6):
            for node in range(10):
                spread[
                    96 * turn + 16 * component + node,
                    packed_row(component, rotations[turn][node]),
                ] = 1.0
    turned = np.concatenate([spread, spread, spread], axis=1)
    packed = np.zeros((464, 256), np.float32)
    for place, matrix in zip(OPERANDS, (traces, volume, raise_up, turned)):
        packed[place : place + matrix.shape[0], : matrix.shape[1]] = matrix
    return jnp.asarray(packed)


def split(values):
    high = values.astype(jnp.bfloat16)
    rest = values - high.astype(jnp.float32)
    middle = rest.astype(jnp.bfloat16)
    low = (rest - middle.astype(jnp.float32)).astype(jnp.bfloat16)
    return high, middle, low


def iota(shape, axis):
    return lax.broadcasted_iota(jnp.int32, shape, axis)


def dot(left, right):
    return jnp.dot(left, right, preferred_element_type=jnp.float32)


def kernel(
    sizes,
    basis_hbm,
    geometry_hbm,
    normals_hbm,
    scale_hbm,
    material_hbm,
    send_list_hbm,
    source_hbm,
    turns_hbm,
    flags_hbm,
    constants_hbm,
    fresh,
    hessenberg,
    stored,
    geometry,
    normals,
    scale,
    material,
    send_list,
    source,
    turns,
    flags,
    constants_wide,
    constants,
    vector,
    field,
    inside,
    around,
    table,
    image,
    flux,
    pick_out,
    pick_in,
    gram,
    held_bound,
    side_row,
    outgoing,
    arrived,
    sums_a,
    sums_b,
    load_sem,
    halo_send,
    halo_recv,
    sum_send,
    sum_recv,
):
    n_gx, n_gy, total = sizes
    kept = basis_hbm.shape[2]
    gx = lax.axis_index("gx")
    gy = lax.axis_index("gy")
    loads = []
    for source_ref, target_ref in (
        (send_list_hbm, send_list),
        (basis_hbm, stored),
        (constants_hbm, constants_wide),
        (source_hbm, source),
        (turns_hbm, turns),
        (flags_hbm, flags),
        (geometry_hbm, geometry),
        (normals_hbm, normals),
        (scale_hbm, scale),
        (material_hbm, material),
    ):
        loads.append(pltpu.make_async_copy(source_ref, target_ref, load_sem.at[len(loads)]))
        loads[-1].start()

    def turned_on(place, step, size):
        place = place + step
        return jnp.where(place >= size, place - size, place)

    partners = []
    for direction in DIRECTIONS:
        partners.append(
            (
                turned_on(gx, (direction // 3 - 1) % n_gx, n_gx),
                turned_on(gy, (direction % 3 - 1) % n_gy, n_gy),
            )
        )
    across = lax.rem(gx, X_CHIPS)
    up = lax.div(gx, X_CHIPS)
    rows_up = n_gx // X_CHIPS
    on_gy = (n_gy, gy, [(gx, turned_on(gy, step, n_gy)) for step in range(1, n_gy)])
    on_gx = (n_gx, gx, [(turned_on(gx, step, n_gx), gy) for step in range(1, n_gx)])
    on_y = (
        rows_up,
        up,
        [(turned_on(gx, X_CHIPS * step, n_gx), gy) for step in range(1, rows_up)],
    )
    on_x = (
        X_CHIPS,
        across,
        [(gx - across + turned_on(across, step, X_CHIPS), gy) for step in range(1, X_CHIPS)],
    )
    narrow = (on_gy, on_gx)
    broad = (on_gy, on_y, on_x)

    barrier = pltpu.get_barrier_semaphore()
    greeted = [partners[index] for index in (0, 2, 5, 7)] + on_gy[2] + on_gx[2]
    for peer in greeted:
        pl.semaphore_signal(barrier, inc=1, device_id=peer, device_id_type=MESH)

    loads[0].wait()
    rows = iota((128, 128), 0)
    for tile in range(4):
        first, second = DIRECTIONS[2 * tile], DIRECTIONS[2 * tile + 1]
        wanted = jnp.concatenate(
            [
                send_list[first // 3, pl.ds(first % 3, 1), :],
                send_list[second // 3, pl.ds(second % 3, 1), :],
            ],
            axis=1,
        )
        for chunk in range(4):
            pick_out[pl.ds(128 * chunk, 128), pl.ds(128 * tile, 128)] = jnp.where(
                rows == wanted - 128 * chunk, 1.0, 0.0
            ).astype(jnp.bfloat16)

    def fill_pick_in():
        for face in range(4):
            named = source[pl.ds(face, 1), :]
            named = jnp.where(named >= 512 + 4 * 64, named - 64, named)
            for chunk in range(8):
                pick_in[pl.ds(128 * chunk, 128), pl.ds(128 * face, 128)] = jnp.where(
                    rows == named - 128 * chunk, 1.0, 0.0
                ).astype(jnp.bfloat16)

    half = iota((32, 128), 1) < 64

    def apply(turn, beside):
        for component in range(6):
            field[pl.ds(0, 20), pl.ds(128 * component, 128)] = vector[component]
        high, middle, low = split(field[...])
        inside[...] = dot(constants[pl.ds(0, 64), pl.ds(0, 96)], jnp.concatenate([high, middle, low], axis=0))
        for component in range(6):
            for face in range(4):
                lane = pl.ds(128 * face, 128)
                column = pl.ds(128 * component, 128)
                table[pl.ds(8 * component, 8), lane] = inside[pl.ds(16 * face, 8), column]
                table[pl.ds(48 + 2 * component, 2), lane] = inside[
                    pl.ds(16 * face + 8, 2), column
                ]
        parts = jnp.concatenate(split(table[...]), axis=0)
        sent = dot(parts, pick_out[...])
        sent = sent[0:64] + sent[64:128] + sent[128:192]
        for tile in range(4):
            top = sent[0:32, 128 * tile : 128 * tile + 128]
            bottom = sent[32:64, 128 * tile : 128 * tile + 128]
            outgoing[turn, 2 * tile] = jnp.where(half, top, pltpu.roll(bottom, 64, 1))
            outgoing[turn, 2 * tile + 1] = jnp.where(half, pltpu.roll(top, 64, 1), bottom)
        for index in range(8):
            pltpu.make_async_remote_copy(
                src_ref=outgoing.at[turn, index],
                dst_ref=arrived.at[turn, 7 - index],
                send_sem=halo_send.at[turn],
                recv_sem=halo_recv.at[turn],
                device_id=partners[index],
                device_id_type=MESH,
            ).start()
        around[...] = dot(
            constants[pl.ds(64, 80), pl.ds(0, 192)],
            jnp.concatenate([high, middle, low, high, high, middle], axis=0)
        )
        beside()
        found = dot(parts, pick_in[pl.ds(0, 512), :])
        pltpu.make_async_copy(arrived.at[turn], arrived.at[turn], halo_recv.at[turn]).wait()
        tops = []
        bottoms = []
        for tile in range(4):
            even = arrived[turn, 2 * tile]
            odd = arrived[turn, 2 * tile + 1]
            tops.append(jnp.where(half, even, pltpu.roll(odd, 64, 1)))
            bottoms.append(jnp.where(half, pltpu.roll(even, 64, 1), odd))
        far = jnp.concatenate(
            [jnp.concatenate(tops, axis=1), jnp.concatenate(bottoms, axis=1)], axis=0
        )
        far = jnp.concatenate(split(far), axis=0)
        found = found + dot(far, pick_in[pl.ds(512, 512), :])
        turned = dot(constants[pl.ds(176, 288), pl.ds(0, 192)], found.astype(jnp.bfloat16))
        for face in range(4):
            lane = slice(128 * face, 128 * face + 128)
            spin = turns[pl.ds(face, 1), :]
            wall = flags[pl.ds(face, 1), :] == 1
            weight = 0.5 * scale[pl.ds(face, 1), :]
            n_x = normals[0, pl.ds(face, 1), :]
            n_y = normals[1, pl.ds(face, 1), :]
            n_z = normals[2, pl.ds(face, 1), :]
            jumps = []
            for component in range(6):
                here = inside[pl.ds(16 * face, 16), pl.ds(128 * component, 128)]
                other = jnp.where(
                    spin == 0,
                    turned[16 * component : 16 * component + 16, lane],
                    jnp.where(
                        spin == 1,
                        turned[96 + 16 * component : 112 + 16 * component, lane],
                        turned[192 + 16 * component : 208 + 16 * component, lane],
                    ),
                )
                other = jnp.where(wall, -here if component < 3 else here, other)
                jumps.append(other - here)
            e_x, e_y, e_z, h_x, h_y, h_z = jumps
            along_e = n_x * e_x + n_y * e_y + n_z * e_z
            along_h = n_x * h_x + n_y * h_y + n_z * h_z
            terms = [
                n_y * h_z - n_z * h_y + e_x - along_e * n_x,
                n_z * h_x - n_x * h_z + e_y - along_e * n_y,
                n_x * h_y - n_y * h_x + e_z - along_e * n_z,
                n_z * e_y - n_y * e_z + h_x - along_h * n_x,
                n_x * e_z - n_z * e_x + h_y - along_h * n_y,
                n_y * e_x - n_x * e_y + h_z - along_h * n_z,
            ]
            for component in range(6):
                flux[pl.ds(16 * face, 16), pl.ds(128 * component, 128)] = (
                    terms[component] * weight
                )
        high, middle, low = split(flux[...])
        lifted = dot(constants[pl.ds(144, 32), :], jnp.concatenate([high, high, middle, low], axis=0))

        def gradient(axis, component):
            column = pl.ds(128 * component, 128)
            return (
                around[pl.ds(0, 20), column] * geometry[pl.ds(axis, 1), :]
                + around[pl.ds(24, 20), column] * geometry[pl.ds(3 + axis, 1), :]
                + around[pl.ds(48, 20), column] * geometry[pl.ds(6 + axis, 1), :]
            )

        for component in range(3):
            after, before = (component + 1) % 3, (component + 2) % 3
            curl_e = gradient(after, before) - gradient(before, after)
            curl_h = gradient(after, 3 + before) - gradient(before, 3 + after)
            raised = lifted[0:20, 128 * component : 128 * component + 128]
            image[component] = (
                material[pl.ds(0, 1), :] * (curl_h + raised)
                - material[pl.ds(2, 1), :] * vector[component]
            )
            raised = lifted[0:20, 384 + 128 * component : 512 + 128 * component]
            image[3 + component] = material[pl.ds(1, 1), :] * (raised - curl_e)

    sub8 = iota((8, 128), 0)
    sub24 = iota((24, 128), 0)
    lane24 = iota((24, 128), 1)
    lane1 = iota((1, 128), 1)
    eye = sub24 == lane24
    sub_k = iota((kept, 128), 0)
    lane_k = iota((kept, 128), 1)

    def inner(vector_ref):
        def some(step, held):
            held = list(held)
            for inner_step in range(4):
                node = 4 * step + inner_step
                for component in range(6):
                    held[component % 3] += (
                        stored[component, node] * vector_ref[component, pl.ds(node, 1), :]
                    )
            return tuple(held)

        zero = jnp.zeros((kept, 128), jnp.float32)
        one, two, three = lax.fori_loop(0, 5, some, (zero, zero, zero))
        column = jnp.sum(one + two + three, axis=1, keepdims=True)
        return jnp.sum(jnp.where(sub_k == lane_k, column, 0.0), axis=0, keepdims=True)

    def to_row(column):
        return jnp.sum(jnp.where(eye, column, 0.0), axis=0, keepdims=True)

    def to_column(row):
        return jnp.sum(jnp.where(eye, row, 0.0), axis=1, keepdims=True)

    def fill_gram():
        def upper(node, held):
            held = list(held)
            for component in range(6):
                tile = stored[component, node]
                for index in range(8):
                    held[index] += tile * stored[component, node, pl.ds(index, 1), :]
            return tuple(held)

        def lower(node, held):
            held = list(held)
            for component in range(6):
                tile = stored[component, node, pl.ds(8, kept - 8), :]
                for index in range(8, 16):
                    held[index - 8] += tile * stored[component, node, pl.ds(index, 1), :]
                tile = tile[8:]
                for index in range(16, kept):
                    held[index - 8] += tile * stored[component, node, pl.ds(index, 1), :]
            return tuple(held)

        def zeros(count, number):
            return (jnp.zeros((count, 128), jnp.float32),) * number

        found = list(lax.fori_loop(0, 20, upper, zeros(kept, 8)))
        found += lax.fori_loop(
            0, 20, lower, zeros(kept - 8, 8) + zeros(kept - 16, kept - 16)
        )
        gram[...] = jnp.zeros((24, 128), jnp.float32)
        for first in (0, 8, 16):
            count = kept - first
            sub = iota((count, 128), 0)
            lane = iota((count, 128), 1)
            held = jnp.zeros((count, 128), jnp.float32)
            for index in range(first, min(first + 8, kept)):
                column = jnp.sum(found[index], axis=1, keepdims=True)
                held = jnp.where(lane == index, column, held)
                row = jnp.sum(jnp.where(sub + first == lane, column, 0.0), axis=0, keepdims=True)
                held = jnp.where((sub == index - first) & (lane >= first), row, held)
            if first == 0:
                gram[pl.ds(0, kept), :] = held
            else:
                old = gram[pl.ds(first, count), :]
                gram[pl.ds(first, count), :] = jnp.where(lane >= first, held, old)

    def begin(value, buffer, groups, which, stage):
        size, mine, peers = groups[stage]
        buffer[stage, mine] = value
        for peer in peers:
            pltpu.make_async_remote_copy(
                src_ref=buffer.at[stage, mine],
                dst_ref=buffer.at[stage, mine],
                send_sem=sum_send.at[which, stage],
                recv_sem=sum_recv.at[which, stage],
                device_id=peer,
                device_id_type=MESH,
            ).start()

    def finish(buffer, groups, which, stage):
        size, mine, peers = groups[stage]
        if size > 1:
            others = buffer.at[stage, pl.ds(0, size - 1)]
            pltpu.make_async_copy(others, others, sum_recv.at[which, stage]).wait()
        values = [buffer[stage, member] for member in range(size)]
        while len(values) > 1:
            values = [sum(values[at : at + 2]) for at in range(0, len(values), 2)]
        return values[0]

    def project(column):
        weights = jnp.broadcast_to(column[0:kept], (kept, 128))
        return [jnp.sum(stored[component] * weights, axis=1) for component in range(6)]

    def whole(values):
        return jnp.sum(jnp.sum(values, axis=0), keepdims=True)

    field[pl.ds(16, 16), :] = jnp.zeros((16, 768), jnp.float32)
    table[pl.ds(56, 8), :] = jnp.zeros((8, 512), jnp.float32)
    held_bound[...] = jnp.ones((1, 128), jnp.float32)
    side_row[...] = jnp.zeros((1, 128), jnp.float32)
    hessenberg[...] = jnp.zeros((2, kept + 2), jnp.float32)
    loads[1].wait()
    loads[2].wait()
    constants[...] = constants_wide[...].astype(jnp.bfloat16)
    for component in range(6):
        vector[component] = stored[component, :, kept - 1, :]
    pl.semaphore_wait(barrier, len(greeted))

    def step(turn, carry):
        first_step = turn == 0
        sums = sums_b.at[turn]

        def beside():
            @pl.when(first_step)
            def _():
                for load in loads[3:]:
                    load.wait()
                fill_pick_in()
                fill_gram()
                packed = (
                    gram[pl.ds(0, 8), :]
                    + pltpu.roll(gram[pl.ds(8, 8), :], 32, 1)
                    + pltpu.roll(gram[pl.ds(16, 8), :], 64, 1)
                )
                begin(packed, sums_a, broad, 2, 0)

            @pl.when(jnp.logical_not(first_step))
            def _():
                side = inner(vector)
                square = whole(vector[...] * vector[...])
                side_row[...] = pltpu.roll(jnp.where(lane1 == kept, square, side), 32, 1)

        apply(turn, beside)

        @pl.when(first_step)
        def _():
            begin(finish(sums_a, broad, 2, 0), sums_a, broad, 2, 1)

        row = inner(image)
        square = whole(image[...] * image[...])
        cross = whole(vector[...] * image[...])
        row = jnp.where(lane1 == 24, square, jnp.where(lane1 == kept, cross, row))
        begin(row + side_row[...], sums, narrow, turn, 0)

        @pl.when(first_step)
        def _():
            begin(finish(sums_a, broad, 2, 1), sums_a, broad, 2, 2)

        begin(finish(sums, narrow, turn, 0), sums, narrow, turn, 1)

        @pl.when(first_step)
        def _():
            packed = finish(sums_a, broad, 2, 2) * (1.0 / total)
            products = jnp.concatenate(
                [packed, pltpu.roll(packed, 96, 1), pltpu.roll(packed, 64, 1)], axis=0
            )
            gram[...] = jnp.where(lane24 < 24, products, 0.0)

        products = gram[...]
        own = jnp.sum(jnp.where(eye, products, 0.0), axis=1, keepdims=True)
        message = finish(sums, narrow, turn, 1) * (1.0 / total)

        bound = held_bound[...][:, 0:1]
        row = jnp.where(lane1 < kept + turn, message, 0.0)
        side = jnp.where(lane1 < kept + 1, pltpu.roll(message, 96, 1), 0.0)
        square = jnp.sum(jnp.where(lane1 == 24, message, 0.0), keepdims=True)
        length = jnp.sum(jnp.where(lane1 == kept, side, 0.0), keepdims=True)
        height = jnp.sqrt(length * (bound * bound) + 1e-06)
        grow = jnp.where(first_step, 1.0, bound / height)
        side = side * jnp.where(lane1 == kept, grow * grow, grow)
        row = row * jnp.where(lane1 == kept, grow * grow, grow)
        extended = kept + turn - 1
        products = jnp.where((lane24 == kept) & (extended == kept), to_column(side), products)
        products = jnp.where((sub24 == kept) & (extended == kept), side, products)
        column = jnp.sum((jnp.where(eye, 2.0, 0.0) - products) * row, axis=1, keepdims=True)
        column_row = to_row(column)

        @pl.when(jnp.logical_not(first_step))
        def _():
            before = hessenberg[pl.ds(0, 1), :]
            hessenberg[pl.ds(0, 1), :] = jnp.where(
                lane1[:, 0:24] == kept, height, before
            )

        square = square * (grow * grow)
        length = square + jnp.sum(
            column * (products * column_row - jnp.where(eye, 2.0, 0.0) * row), keepdims=True
        )
        height = jnp.sqrt(jnp.maximum(length, 0.0) + 1e-06)
        bound = jnp.sum(jnp.abs(column) * jnp.sqrt(own), keepdims=True) + jnp.sqrt(square) + 1e-3
        held_bound[...] = jnp.broadcast_to(bound, (1, 128))
        shrink = 1.0 / jnp.where(first_step, bound, height)
        taken = project(column * shrink)
        on_own = column[kept : kept + 1] * (grow * shrink)
        for component in range(6):
            current = vector[component]
            new = image[component] * (grow * shrink) - current * on_own - taken[component]
            fresh[0, component] = current * grow
            fresh[1, component] = new
            vector[component] = new
        hessenberg[pl.ds(turn, 1), :] = jnp.where(
            lane1 == kept + 1, jnp.where(first_step, 0.0, height), column_row
        )[:, 0:24]
        return carry

    lax.fori_loop(0, 2, step, 0)
    for turn in range(2):
        pltpu.make_async_copy(outgoing.at[turn], outgoing.at[turn], halo_send.at[turn]).wait()
    for which in range(3):
        for stage, (size, _, _) in enumerate(broad if which == 2 else narrow):
            if size > 1:
                buffer = sums_a if which == 2 else sums_b.at[which]
                others = buffer.at[stage, pl.ds(0, size - 1)]
                pltpu.make_async_copy(others, others, sum_send.at[which, stage]).wait()


def body(
    n_gx,
    n_gy,
    basis,
    geometry,
    face_normals,
    face_scale,
    material,
    send_list,
    neighbour_source,
    node_rotation,
    boundary_flag,
):
    kept, components, nodes, local_count = basis.shape
    total = float(components * nodes * local_count * n_gx * n_gy)
    f32, bf16 = jnp.float32, jnp.bfloat16
    anywhere = pl.BlockSpec(memory_space=pl.ANY)
    vmem = pl.BlockSpec(memory_space=pltpu.VMEM)
    return pl.pallas_call(
        functools.partial(kernel, (n_gx, n_gy, total)),
        out_shape=(
            pltpu.VMEM((2, components, nodes, local_count), f32),
            pltpu.VMEM((2, kept + 2), f32),
        ),
        in_specs=[anywhere] * 10,
        out_specs=(vmem, vmem),
        scratch_shapes=[
            pltpu.VMEM((components, nodes, kept, local_count), f32),
            pltpu.VMEM(geometry.shape, f32),
            pltpu.VMEM(face_normals.shape, f32),
            pltpu.VMEM(face_scale.shape, f32),
            pltpu.VMEM(material.shape, f32),
            pltpu.VMEM(send_list.shape, jnp.int32),
            pltpu.VMEM(neighbour_source.shape, jnp.int32),
            pltpu.VMEM(node_rotation.shape, jnp.int32),
            pltpu.VMEM(boundary_flag.shape, jnp.int32),
            pltpu.VMEM((464, 256), f32),
            pltpu.VMEM((464, 256), bf16),
            pltpu.VMEM((components, nodes, local_count), f32),
            pltpu.VMEM((32, 768), f32),
            pltpu.VMEM((64, 768), f32),
            pltpu.VMEM((80, 768), f32),
            pltpu.VMEM((64, 512), f32),
            pltpu.VMEM((components, nodes, local_count), f32),
            pltpu.VMEM((64, 768), f32),
            pltpu.VMEM((512, 512), bf16),
            pltpu.VMEM((1024, 512), bf16),
            pltpu.VMEM((24, 128), f32),
            pltpu.VMEM((1, 128), f32),
            pltpu.VMEM((1, 128), f32),
            pltpu.VMEM((2, 8, 32, 128), f32),
            pltpu.VMEM((2, 8, 32, 128), f32),
            pltpu.VMEM((3, max(n_gx // X_CHIPS, n_gy, X_CHIPS), 8, 128), f32),
            pltpu.VMEM((2, 2, max(n_gx, n_gy), 1, 128), f32),
            pltpu.SemaphoreType.DMA((10,)),
            pltpu.SemaphoreType.DMA((2,)),
            pltpu.SemaphoreType.DMA((2,)),
            pltpu.SemaphoreType.DMA((3, 3)),
            pltpu.SemaphoreType.DMA((3, 3)),
        ],
        compiler_params=pltpu.CompilerParams(
            collective_id=0, has_side_effects=True, vmem_limit_bytes=32 * 1024 * 1024
        ),
    )(
        *[
            pltpu.with_memory_space_constraint(operand, pltpu.HBM)
            for operand in (
                jnp.transpose(basis, (1, 2, 0, 3)),
                geometry,
                face_normals,
                face_scale,
                material,
                send_list,
                neighbour_source,
                node_rotation,
                boundary_flag,
                left_operands(),
            )
        ]
    )


def solution(mesh):
    placed = (
        P(None, None, None, ("gx", "gy")),
        P(None, ("gx", "gy")),
        P(None, None, ("gx", "gy")),
        P(None, ("gx", "gy")),
        P(None, ("gx", "gy")),
        P("gx", "gy", None),
        P(None, ("gx", "gy")),
        P(None, ("gx", "gy")),
        P(None, ("gx", "gy")),
    )
    return jax.shard_map(
        functools.partial(body, mesh.shape["gx"], mesh.shape["gy"]),
        mesh=mesh,
        in_specs=placed,
        out_specs=(P(None, None, None, ("gx", "gy")), P()),
        check_vma=False,
    )
```

time: 690 us -> 53.6 us (0.08)
  blocking collectives: 579 us -> 0 us
  Pallas kernels: 0 us -> 51.5 us
  starting transfers between devices: 28.8 us -> 0 us
  local copies, waits for them, and re-layouts: 29.7 us -> 1.27 us
  other arithmetic: 25.2 us -> 0 us
  matrix products: 18.8 us -> 0 us
    psum x6 -> x0, blocking collectives: 579 us -> none  [the longest x2 200 us: body(): first_v, first_n = lax.psum((part_v, part_n), ('gx', 'gy'))]
    pallas_call x0 -> x1, Pallas kernels: none -> 51.5 us  [body(): pl.pallas_call(functools.partial(kernel, (n_gx, n_gy, total)), out_shape=...]
    ppermute x8 -> x0, starting transfers between devices: 28.8 us -> none  [the longest x4 14.4 us: padded_2(): lax.ppermute(lax.slice_in_dim(block, 0, width, axis=dim), axis, backward)]
    dot_general x20 -> x0, matrix products: 18.8 us -> none  [the longest x4 5.95 us: body(): part_v = jnp.dot(stacked, image, precision=highest)]
    slice x15 -> x0, local copies, waits for them, and re-layouts: 11.5 us -> none  [the longest x5 4.96 us: flux_terms(): other_e = jnp.where(wall, -inside[:3], other[:3])]
    gather x14 -> x0, local copies, waits for them, and re-layouts: 11.4 us -> none  [the longest x2 3.86 us: body(): outgoing = jnp.take(inside, outgoing_index, axis=1)]
    sub x12 -> x0, other arithmetic: 7.55 us -> none  [the longest x2 1.89 us: flux_terms(): jump_e = other_e - inside[:3]]
  transfers between devices with their start and end apart: 8 -> 0, of which waited for: 3 -> 0; matrix products, arithmetic and copies ran while one was open for 3% -> 0% of each run, Pallas kernels for 0% -> 0%
where the time goes in v1:
time: 53.6 us; the launch traced here: 53.4 us
  Pallas kernels  51.5 us (96%)
  local copies, waits for them, and re-layouts  1.27 us (2%)
  between operations  0.64 us (1%)
    pallas_call x1, Pallas kernels, body(): pl.pallas_call(functools.partial(kernel, (n_gx, n_gy, total)), out_shape=...  51.5 us

profile of v1, /device:TPU:1, one launch (start us, length us, event | category | flops | bytes accessed | tf_op | source)
XLA Modules:
  0.0 53.4 jit_solution(6300961312021897017)
XLA Ops:
  0.6 51.5 %shard_map.113 = (f32[2,6,20,128]{3,2,1,0:T(8,128)S(1)}, f32[2,24]{1,0:T(2,128)S(1)}) custom-call(f32[6,20,22,128]{3,2,1,0:T(8,128)} %bitcast.1, f32[9,128]{1,0:T(8,128)} %geometry_hbm.1, f32[3,4,128]{2,1,0:T(4,128)} %normals_hbm.1, f32[4,128]{1,0:T(4,128)} %scale_hbm.1, f32[3,128]{1,0:T(4,128)} %material_hbm.1, s32[3,3,64]{2,1,0:T(4,128)} %send_list_hbm.1, ...), custom_call_target="tpu_custom_call" | custom-call | tf_op jit(solution)/shard_map/pallas_call | solution.py:658
  52.2 0.7 %copy.12 = f32[2,6,20,128]{3,0,2,1:T(2,128)} copy(f32[2,6,20,128]{3,2,1,0:T(8,128)S(1)} %get-tuple-element.2) | data formatting | bytes 245760 | tf_op jit(solution)/shard_map/pallas_call | solution.py:658
  52.9 0.6 %copy.14 = f32[2,24]{1,0:T(2,128)} copy(f32[2,24]{1,0:T(2,128)S(1)} %get-tuple-element.5) | data formatting | bytes 384

commit v2 on v1

--- a/solution.py
+++ b/solution.py
@@ -204,6 +204,7 @@
     inside,
     around,
     table,
+    parts,
     image,
     flux,
     pick_out,
@@ -211,6 +212,7 @@
     gram,
     held_bound,
     side_row,
+    work,
     outgoing,
     arrived,
     sums_a,
@@ -256,12 +258,16 @@
     across = lax.rem(gx, X_CHIPS)
     up = lax.div(gx, X_CHIPS)
     rows_up = n_gx // X_CHIPS
-    on_gy = (n_gy, gy, [(gx, turned_on(gy, step, n_gy)) for step in range(1, n_gy)])
-    on_gx = (n_gx, gx, [(turned_on(gx, step, n_gx), gy) for step in range(1, n_gx)])
+
+    def farthest_first(size):
+        return sorted(range(1, size), key=lambda step: -min(step, size - step))
+
+    on_gy = (n_gy, gy, [(gx, turned_on(gy, step, n_gy)) for step in farthest_first(n_gy)])
+    on_gx = (n_gx, gx, [(turned_on(gx, step, n_gx), gy) for step in farthest_first(n_gx)])
     on_y = (
         rows_up,
         up,
-        [(turned_on(gx, X_CHIPS * step, n_gx), gy) for step in range(1, rows_up)],
+        [(turned_on(gx, X_CHIPS * step, n_gx), gy) for step in farthest_first(rows_up)],
     )
     on_x = (
         X_CHIPS,
@@ -269,7 +275,7 @@
         [(gx - across + turned_on(across, step, X_CHIPS), gy) for step in range(1, X_CHIPS)],
     )
     narrow = (on_gy, on_gx)
-    broad = (on_gy, on_y, on_x)
+    broad = (on_y, on_gy, on_x)
 
     barrier = pltpu.get_barrier_semaphore()
     greeted = [partners[index] for index in (0, 2, 5, 7)] + on_gy[2] + on_gx[2]
@@ -303,7 +309,7 @@
 
     half = iota((32, 128), 1) < 64
 
-    def apply(turn, beside):
+    def prepare(turn):
         for component in range(6):
             field[pl.ds(0, 20), pl.ds(128 * component, 128)] = vector[component]
         high, middle, low = split(field[...])
@@ -316,15 +322,17 @@
                 table[pl.ds(48 + 2 * component, 2), lane] = inside[
                     pl.ds(16 * face + 8, 2), column
                 ]
-        parts = jnp.concatenate(split(table[...]), axis=0)
-        sent = dot(parts, pick_out[...])
+        parts[...] = jnp.concatenate(split(table[...]), axis=0)
+        sent = dot(parts[...], pick_out[...])
         sent = sent[0:64] + sent[64:128] + sent[128:192]
         for tile in range(4):
             top = sent[0:32, 128 * tile : 128 * tile + 128]
             bottom = sent[32:64, 128 * tile : 128 * tile + 128]
             outgoing[turn, 2 * tile] = jnp.where(half, top, pltpu.roll(bottom, 64, 1))
             outgoing[turn, 2 * tile + 1] = jnp.where(half, pltpu.roll(top, 64, 1), bottom)
-        for index in range(8):
+
+    def apply(turn, beside):
+        for index in (0, 2, 5, 7, 1, 6, 3, 4):
             pltpu.make_async_remote_copy(
                 src_ref=outgoing.at[turn, index],
                 dst_ref=arrived.at[turn, 7 - index],
@@ -333,12 +341,13 @@
                 device_id=partners[index],
                 device_id_type=MESH,
             ).start()
+        high, middle, low = split(field[...])
         around[...] = dot(
             constants[pl.ds(64, 80), pl.ds(0, 192)],
             jnp.concatenate([high, middle, low, high, high, middle], axis=0)
         )
         beside()
-        found = dot(parts, pick_in[pl.ds(0, 512), :])
+        found = dot(parts[...], pick_in[pl.ds(0, 512), :])
         pltpu.make_async_copy(arrived.at[turn], arrived.at[turn], halo_recv.at[turn]).wait()
         tops = []
         bottoms = []
@@ -418,10 +427,8 @@
     lane24 = iota((24, 128), 1)
     lane1 = iota((1, 128), 1)
     eye = sub24 == lane24
-    sub_k = iota((kept, 128), 0)
-    lane_k = iota((kept, 128), 1)
-
-    def inner(vector_ref):
+
+    def inner(vector_ref, *pairs):
         def some(step, held):
             held = list(held)
             for inner_step in range(4):
@@ -433,9 +440,12 @@
             return tuple(held)
 
         zero = jnp.zeros((kept, 128), jnp.float32)
+        for place, (left, right) in enumerate(pairs):
+            partial = jnp.sum(left[...] * right[...], axis=0)
+            work[pl.ds(kept + place, 1), :] = jnp.sum(partial, axis=0, keepdims=True)
         one, two, three = lax.fori_loop(0, 5, some, (zero, zero, zero))
-        column = jnp.sum(one + two + three, axis=1, keepdims=True)
-        return jnp.sum(jnp.where(sub_k == lane_k, column, 0.0), axis=0, keepdims=True)
+        work[pl.ds(0, kept), :] = one + two + three
+        return to_row(jnp.sum(work[...], axis=1, keepdims=True))
 
     def to_row(column):
         return jnp.sum(jnp.where(eye, column, 0.0), axis=0, keepdims=True)
@@ -514,19 +524,18 @@
         weights = jnp.broadcast_to(column[0:kept], (kept, 128))
         return [jnp.sum(stored[component] * weights, axis=1) for component in range(6)]
 
-    def whole(values):
-        return jnp.sum(jnp.sum(values, axis=0), keepdims=True)
-
     field[pl.ds(16, 16), :] = jnp.zeros((16, 768), jnp.float32)
     table[pl.ds(56, 8), :] = jnp.zeros((8, 512), jnp.float32)
     held_bound[...] = jnp.ones((1, 128), jnp.float32)
     side_row[...] = jnp.zeros((1, 128), jnp.float32)
+    work[...] = jnp.zeros((24, 128), jnp.float32)
     hessenberg[...] = jnp.zeros((2, kept + 2), jnp.float32)
     loads[1].wait()
     loads[2].wait()
     constants[...] = constants_wide[...].astype(jnp.bfloat16)
     for component in range(6):
         vector[component] = stored[component, :, kept - 1, :]
+    prepare(0)
     pl.semaphore_wait(barrier, len(greeted))
 
     def step(turn, carry):
@@ -549,30 +558,22 @@
 
             @pl.when(jnp.logical_not(first_step))
             def _():
-                side = inner(vector)
-                square = whole(vector[...] * vector[...])
-                side_row[...] = pltpu.roll(jnp.where(lane1 == kept, square, side), 32, 1)
+                side_row[...] = pltpu.roll(inner(vector, (vector, vector)), 32, 1)
 
         apply(turn, beside)
+
+        row = inner(image, (vector, image), (image, image))
+        begin(row + side_row[...], sums, narrow, turn, 0)
 
         @pl.when(first_step)
         def _():
             begin(finish(sums_a, broad, 2, 0), sums_a, broad, 2, 1)
 
-        row = inner(image)
-        square = whole(image[...] * image[...])
-        cross = whole(vector[...] * image[...])
-        row = jnp.where(lane1 == 24, square, jnp.where(lane1 == kept, cross, row))
-        begin(row + side_row[...], sums, narrow, turn, 0)
+        begin(finish(sums, narrow, turn, 0), sums, narrow, turn, 1)
 
         @pl.when(first_step)
         def _():
             begin(finish(sums_a, broad, 2, 1), sums_a, broad, 2, 2)
-
-        begin(finish(sums, narrow, turn, 0), sums, narrow, turn, 1)
-
-        @pl.when(first_step)
-        def _():
             packed = finish(sums_a, broad, 2, 2) * (1.0 / total)
             products = jnp.concatenate(
                 [packed, pltpu.roll(packed, 96, 1), pltpu.roll(packed, 64, 1)], axis=0
@@ -586,7 +587,7 @@
         bound = held_bound[...][:, 0:1]
         row = jnp.where(lane1 < kept + turn, message, 0.0)
         side = jnp.where(lane1 < kept + 1, pltpu.roll(message, 96, 1), 0.0)
-        square = jnp.sum(jnp.where(lane1 == 24, message, 0.0), keepdims=True)
+        square = jnp.sum(jnp.where(lane1 == kept + 1, message, 0.0), keepdims=True)
         length = jnp.sum(jnp.where(lane1 == kept, side, 0.0), keepdims=True)
         height = jnp.sqrt(length * (bound * bound) + 1e-06)
         grow = jnp.where(first_step, 1.0, bound / height)
@@ -613,17 +614,22 @@
         bound = jnp.sum(jnp.abs(column) * jnp.sqrt(own), keepdims=True) + jnp.sqrt(square) + 1e-3
         held_bound[...] = jnp.broadcast_to(bound, (1, 128))
         shrink = 1.0 / jnp.where(first_step, bound, height)
-        taken = project(column * shrink)
-        on_own = column[kept : kept + 1] * (grow * shrink)
+        taken = project(column)
+        on_own = column[kept : kept + 1] * grow
         for component in range(6):
             current = vector[component]
-            new = image[component] * (grow * shrink) - current * on_own - taken[component]
+            new = (image[component] * grow - current * on_own - taken[component]) * shrink
             fresh[0, component] = current * grow
             fresh[1, component] = new
             vector[component] = new
         hessenberg[pl.ds(turn, 1), :] = jnp.where(
             lane1 == kept + 1, jnp.where(first_step, 0.0, height), column_row
         )[:, 0:24]
+
+        @pl.when(first_step)
+        def _():
+            prepare(1)
+
         return carry
 
     lax.fori_loop(0, 2, step, 0)
@@ -680,6 +686,7 @@
             pltpu.VMEM((64, 768), f32),
             pltpu.VMEM((80, 768), f32),
             pltpu.VMEM((64, 512), f32),
+            pltpu.VMEM((192, 512), bf16),
             pltpu.VMEM((components, nodes, local_count), f32),
             pltpu.VMEM((64, 768), f32),
             pltpu.VMEM((512, 512), bf16),
@@ -687,6 +694,7 @@
             pltpu.VMEM((24, 128), f32),
             pltpu.VMEM((1, 128), f32),
             pltpu.VMEM((1, 128), f32),
+            pltpu.VMEM((24, 128), f32),
             pltpu.VMEM((2, 8, 32, 128), f32),
             pltpu.VMEM((2, 8, 32, 128), f32),
             pltpu.VMEM((3, max(n_gx // X_CHIPS, n_gy, X_CHIPS), 8, 128), f32),

time: 53.6 us -> 51 us (0.951)
  Pallas kernels: 51.5 us -> 48.9 us
    pallas_call x1, Pallas kernels: 51.5 us -> 48.9 us  [body(): pl.pallas_call(functools.partial(kernel, (n_gx, n_gy, total)), out_shape=...]
where the time goes in v2:
time: 51 us; the launch traced here: 50.9 us
  Pallas kernels  48.9 us (96%)
  local copies, waits for them, and re-layouts  1.27 us (2%)
  between operations  0.64 us (1%)
    pallas_call x1, Pallas kernels, body(): pl.pallas_call(functools.partial(kernel, (n_gx, n_gy, total)), out_shape=...  48.9 us

profile of v2, /device:TPU:1, one launch (start us, length us, event | category | flops | bytes accessed | tf_op | source)
XLA Modules:
  0.0 50.9 jit_solution(4381188472975419259)
XLA Ops:
  0.6 48.9 %shard_map.113 = (f32[2,6,20,128]{3,2,1,0:T(8,128)S(1)}, f32[2,24]{1,0:T(2,128)S(1)}) custom-call(f32[6,20,22,128]{3,2,1,0:T(8,128)} %bitcast.1, f32[9,128]{1,0:T(8,128)} %geometry_hbm.1, f32[3,4,128]{2,1,0:T(4,128)} %normals_hbm.1, f32[4,128]{1,0:T(4,128)} %scale_hbm.1, f32[3,128]{1,0:T(4,128)} %material_hbm.1, s32[3,3,64]{2,1,0:T(4,128)} %send_list_hbm.1, ...), custom_call_target="tpu_custom_call" | custom-call | tf_op jit(solution)/shard_map/pallas_call | solution.py:664
  49.6 0.7 %copy.12 = f32[2,6,20,128]{3,0,2,1:T(2,128)} copy(f32[2,6,20,128]{3,2,1,0:T(8,128)S(1)} %get-tuple-element.2) | data formatting | bytes 245760 | tf_op jit(solution)/shard_map/pallas_call | solution.py:664
  50.3 0.6 %copy.14 = f32[2,24]{1,0:T(2,128)} copy(f32[2,24]{1,0:T(2,128)S(1)} %get-tuple-element.5) | data formatting | bytes 384

commit v3 on v2

--- a/solution.py
+++ b/solution.py
@@ -213,6 +213,8 @@
     held_bound,
     side_row,
     work,
+    spread,
+    taken,
     outgoing,
     arrived,
     sums_a,
@@ -227,11 +229,16 @@
     kept = basis_hbm.shape[2]
     gx = lax.axis_index("gx")
     gy = lax.axis_index("gy")
+    last = kept // 8 * 8
+    block = (slice(None), slice(None), pl.ds(last, kept - last))
+    rest = (slice(None), slice(None), pl.ds(0, last))
     loads = []
     for source_ref, target_ref in (
         (send_list_hbm, send_list),
-        (basis_hbm, stored),
-        (constants_hbm, constants_wide),
+        (basis_hbm.at[block], stored.at[block]),
+        (constants_hbm.at[pl.ds(0, 64)], constants_wide.at[pl.ds(0, 64)]),
+        (constants_hbm.at[pl.ds(64, 400)], constants_wide.at[pl.ds(64, 400)]),
+        (basis_hbm.at[rest], stored.at[rest]),
         (source_hbm, source),
         (turns_hbm, turns),
         (flags_hbm, flags),
@@ -241,7 +248,8 @@
         (material_hbm, material),
     ):
         loads.append(pltpu.make_async_copy(source_ref, target_ref, load_sem.at[len(loads)]))
-        loads[-1].start()
+    for load in loads[:3]:
+        load.start()
 
     def turned_on(place, step, size):
         place = place + step
@@ -278,7 +286,9 @@
     broad = (on_y, on_gy, on_x)
 
     barrier = pltpu.get_barrier_semaphore()
-    greeted = [partners[index] for index in (0, 2, 5, 7)] + on_gy[2] + on_gx[2]
+    greeted = list(partners)
+    greeted += [(gx, turned_on(gy, step, n_gy)) for step in range(2, n_gy - 1)]
+    greeted += [(turned_on(gx, step, n_gx), gy) for step in range(2, n_gx - 1)]
     for peer in greeted:
         pl.semaphore_signal(barrier, inc=1, device_id=peer, device_id_type=MESH)
 
@@ -522,7 +532,22 @@
 
     def project(column):
         weights = jnp.broadcast_to(column[0:kept], (kept, 128))
-        return [jnp.sum(stored[component] * weights, axis=1) for component in range(6)]
+
+        def one(component, carry):
+            for node in range(20):
+                product = stored[component, node] * weights
+                short = jnp.concatenate(
+                    [product[16:kept], jnp.zeros((24 - kept, 128), jnp.float32)], axis=0
+                )
+                spread[component, pl.ds(8 * node, 8), :] = product[0:8] + product[8:16] + short
+            return carry
+
+        lax.fori_loop(0, 6, one, 0)
+        for component in range(6):
+            parts_of = [spread[component, pl.ds(at, 20, stride=8), :] for at in range(8)]
+            while len(parts_of) > 1:
+                parts_of = [sum(parts_of[at : at + 2]) for at in range(0, len(parts_of), 2)]
+            taken[component] = parts_of[0]
 
     field[pl.ds(16, 16), :] = jnp.zeros((16, 768), jnp.float32)
     table[pl.ds(56, 8), :] = jnp.zeros((8, 512), jnp.float32)
@@ -532,10 +557,15 @@
     hessenberg[...] = jnp.zeros((2, kept + 2), jnp.float32)
     loads[1].wait()
     loads[2].wait()
-    constants[...] = constants_wide[...].astype(jnp.bfloat16)
+    for load in loads[3:]:
+        load.start()
+    constants[pl.ds(0, 64), :] = constants_wide[pl.ds(0, 64), :].astype(jnp.bfloat16)
     for component in range(6):
         vector[component] = stored[component, :, kept - 1, :]
     prepare(0)
+    for load in loads[3:]:
+        load.wait()
+    constants[pl.ds(64, 400), :] = constants_wide[pl.ds(64, 400), :].astype(jnp.bfloat16)
     pl.semaphore_wait(barrier, len(greeted))
 
     def step(turn, carry):
@@ -545,8 +575,6 @@
         def beside():
             @pl.when(first_step)
             def _():
-                for load in loads[3:]:
-                    load.wait()
                 fill_pick_in()
                 fill_gram()
                 packed = (
@@ -614,7 +642,7 @@
         bound = jnp.sum(jnp.abs(column) * jnp.sqrt(own), keepdims=True) + jnp.sqrt(square) + 1e-3
         held_bound[...] = jnp.broadcast_to(bound, (1, 128))
         shrink = 1.0 / jnp.where(first_step, bound, height)
-        taken = project(column)
+        project(column)
         on_own = column[kept : kept + 1] * grow
         for component in range(6):
             current = vector[component]
@@ -695,11 +723,13 @@
             pltpu.VMEM((1, 128), f32),
             pltpu.VMEM((1, 128), f32),
             pltpu.VMEM((24, 128), f32),
+            pltpu.VMEM((components, 8 * nodes, local_count), f32),
+            pltpu.VMEM((components, nodes, local_count), f32),
             pltpu.VMEM((2, 8, 32, 128), f32),
             pltpu.VMEM((2, 8, 32, 128), f32),
             pltpu.VMEM((3, max(n_gx // X_CHIPS, n_gy, X_CHIPS), 8, 128), f32),
             pltpu.VMEM((2, 2, max(n_gx, n_gy), 1, 128), f32),
-            pltpu.SemaphoreType.DMA((10,)),
+            pltpu.SemaphoreType.DMA((12,)),
             pltpu.SemaphoreType.DMA((2,)),
             pltpu.SemaphoreType.DMA((2,)),
             pltpu.SemaphoreType.DMA((3, 3)),

time: 51 us -> 51.4 us (level)
  no operation moved by 1% of the time
where the time goes in v3:
time: 51.4 us; the launch traced here: 51.2 us
  Pallas kernels  49.3 us (96%)
  local copies, waits for them, and re-layouts  1.27 us (2%)
  between operations  0.64 us (1%)
    pallas_call x1, Pallas kernels, body(): pl.pallas_call(functools.partial(kernel, (n_gx, n_gy, total)), out_shape=...  49.3 us

profile of v3, /device:TPU:1, one launch (start us, length us, event | category | flops | bytes accessed | tf_op | source)
XLA Modules:
  0.0 51.2 jit_solution(991443133927592616)
XLA Ops:
  0.6 49.3 %shard_map.113 = (f32[2,6,20,128]{3,2,1,0:T(8,128)S(1)}, f32[2,24]{1,0:T(2,128)S(1)}) custom-call(f32[6,20,22,128]{3,2,1,0:T(8,128)} %bitcast.1, f32[9,128]{1,0:T(8,128)} %geometry_hbm.1, f32[3,4,128]{2,1,0:T(4,128)} %normals_hbm.1, f32[4,128]{1,0:T(4,128)} %scale_hbm.1, f32[3,128]{1,0:T(4,128)} %material_hbm.1, s32[3,3,64]{2,1,0:T(4,128)} %send_list_hbm.1, ...), custom_call_target="tpu_custom_call" | custom-call | tf_op jit(solution)/shard_map/pallas_call | solution.py:692
  49.9 0.7 %copy.12 = f32[2,6,20,128]{3,0,2,1:T(2,128)} copy(f32[2,6,20,128]{3,2,1,0:T(8,128)S(1)} %get-tuple-element.2) | data formatting | bytes 245760 | tf_op jit(solution)/shard_map/pallas_call | solution.py:692
  50.6 0.6 %copy.14 = f32[2,24]{1,0:T(2,128)} copy(f32[2,24]{1,0:T(2,128)S(1)} %get-tuple-element.5) | data formatting | bytes 384

commit v4 on v3

--- a/solution.py
+++ b/solution.py
@@ -11,7 +11,7 @@
 
 MESH = pl.DeviceIdType.MESH
 X_CHIPS = 4
-OPERANDS = (0, 64, 144, 176)
+OPERANDS = (0, 80, 112)
 DIRECTIONS = (0, 1, 2, 3, 5, 6, 7, 8)
 
 
@@ -126,11 +126,6 @@
 
 def left_operands():
     derivs, lift, face_nodes, rotations = element_tables()
-    pick = np.zeros((64, 32), np.float32)
-    for face in range(4):
-        for node in range(10):
-            pick[16 * face + node, face_nodes[node, face]] = 1.0
-    traces = np.concatenate([pick, pick, pick], axis=1)
     stack = np.zeros((3, 80, 32), np.float32)
     for index, part in enumerate(bf16_parts(derivs)):
         for axis in range(3):
@@ -143,17 +138,17 @@
             for node in range(10):
                 blocks[index, :20, 16 * face + node] = part[:, node * 4 + face].astype(np.float32)
     raise_up = np.concatenate([blocks[0], blocks[1], blocks[0], blocks[0]], axis=1)
-    spread = np.zeros((288, 64), np.float32)
+    spread = np.zeros((192, 64), np.float32)
     for turn in range(3):
         for component in range(6):
             for node in range(10):
                 spread[
-                    96 * turn + 16 * component + node,
+                    64 * turn + packed_row(component, node),
                     packed_row(component, rotations[turn][node]),
                 ] = 1.0
     turned = np.concatenate([spread, spread, spread], axis=1)
-    packed = np.zeros((464, 256), np.float32)
-    for place, matrix in zip(OPERANDS, (traces, volume, raise_up, turned)):
+    packed = np.zeros((304, 256), np.float32)
+    for place, matrix in zip(OPERANDS, (volume, raise_up, turned)):
         packed[place : place + matrix.shape[0], : matrix.shape[1]] = matrix
     return jnp.asarray(packed)
 
@@ -201,14 +196,14 @@
     constants,
     vector,
     field,
-    inside,
     around,
     table,
-    parts,
+    others,
+    rotated,
     image,
     flux,
-    pick_out,
-    pick_in,
+    index_out,
+    index_in,
     gram,
     held_bound,
     side_row,
@@ -225,7 +220,7 @@
     sum_send,
     sum_recv,
 ):
-    n_gx, n_gy, total = sizes
+    n_gx, n_gy, total, face_nodes = sizes
     kept = basis_hbm.shape[2]
     gx = lax.axis_index("gx")
     gy = lax.axis_index("gy")
@@ -236,8 +231,7 @@
     for source_ref, target_ref in (
         (send_list_hbm, send_list),
         (basis_hbm.at[block], stored.at[block]),
-        (constants_hbm.at[pl.ds(0, 64)], constants_wide.at[pl.ds(0, 64)]),
-        (constants_hbm.at[pl.ds(64, 400)], constants_wide.at[pl.ds(64, 400)]),
+        (constants_hbm, constants_wide),
         (basis_hbm.at[rest], stored.at[rest]),
         (source_hbm, source),
         (turns_hbm, turns),
@@ -248,7 +242,7 @@
         (material_hbm, material),
     ):
         loads.append(pltpu.make_async_copy(source_ref, target_ref, load_sem.at[len(loads)]))
-    for load in loads[:3]:
+    for load in loads[:2]:
         load.start()
 
     def turned_on(place, step, size):
@@ -293,144 +287,152 @@
         pl.semaphore_signal(barrier, inc=1, device_id=peer, device_id_type=MESH)
 
     loads[0].wait()
-    rows = iota((128, 128), 0)
     for tile in range(4):
         first, second = DIRECTIONS[2 * tile], DIRECTIONS[2 * tile + 1]
-        wanted = jnp.concatenate(
+        index_out[pl.ds(tile, 1), :] = jnp.concatenate(
             [
                 send_list[first // 3, pl.ds(first % 3, 1), :],
                 send_list[second // 3, pl.ds(second % 3, 1), :],
             ],
             axis=1,
         )
-        for chunk in range(4):
-            pick_out[pl.ds(128 * chunk, 128), pl.ds(128 * tile, 128)] = jnp.where(
-                rows == wanted - 128 * chunk, 1.0, 0.0
-            ).astype(jnp.bfloat16)
-
-    def fill_pick_in():
-        for face in range(4):
-            named = source[pl.ds(face, 1), :]
-            named = jnp.where(named >= 512 + 4 * 64, named - 64, named)
-            for chunk in range(8):
-                pick_in[pl.ds(128 * chunk, 128), pl.ds(128 * face, 128)] = jnp.where(
-                    rows == named - 128 * chunk, 1.0, 0.0
-                ).astype(jnp.bfloat16)
+
+    def pick(found, sources, index, first):
+        lane = jnp.broadcast_to(jnp.bitwise_and(index, 127), (64, 128))
+        tile = jnp.broadcast_to(jnp.right_shift(index, 7), (64, 128))
+        for place, values in enumerate(sources):
+            picked = jnp.take_along_axis(values, lane, axis=1, mode="promise_in_bounds")
+            found = picked if found is None else jnp.where(tile == first + place, picked, found)
+        return found
 
     half = iota((32, 128), 1) < 64
 
-    def prepare(turn):
+    def prepare(turn, greeting):
+        for component in range(6):
+            for face in range(4):
+                for node in range(10):
+                    row = pl.ds(packed_row(component, node), 1)
+                    table[row, pl.ds(128 * face, 128)] = vector[
+                        component, pl.ds(int(face_nodes[node, face]), 1), :
+                    ]
+        greeting()
+        sources = [table[:, pl.ds(128 * tile, 128)] for tile in range(4)]
+        for tile in (0, 3, 1, 2):
+            sent = pick(None, sources, index_out[pl.ds(tile, 1), :], 0)
+            top = sent[0:32]
+            bottom = sent[32:64]
+            outgoing[turn, 2 * tile] = jnp.where(half, top, pltpu.roll(bottom, 64, 1))
+            outgoing[turn, 2 * tile + 1] = jnp.where(half, pltpu.roll(top, 64, 1), bottom)
+            for index in (2 * tile, 2 * tile + 1):
+                pltpu.make_async_remote_copy(
+                    src_ref=outgoing.at[turn, index],
+                    dst_ref=arrived.at[turn, 7 - index],
+                    send_sem=halo_send.at[turn],
+                    recv_sem=halo_recv.at[turn],
+                    device_id=partners[index],
+                    device_id_type=MESH,
+                ).start()
+
+    def apply(turn, ready, beside):
+        ready()
         for component in range(6):
             field[pl.ds(0, 20), pl.ds(128 * component, 128)] = vector[component]
         high, middle, low = split(field[...])
-        inside[...] = dot(constants[pl.ds(0, 64), pl.ds(0, 96)], jnp.concatenate([high, middle, low], axis=0))
-        for component in range(6):
-            for face in range(4):
-                lane = pl.ds(128 * face, 128)
-                column = pl.ds(128 * component, 128)
-                table[pl.ds(8 * component, 8), lane] = inside[pl.ds(16 * face, 8), column]
-                table[pl.ds(48 + 2 * component, 2), lane] = inside[
-                    pl.ds(16 * face + 8, 2), column
-                ]
-        parts[...] = jnp.concatenate(split(table[...]), axis=0)
-        sent = dot(parts[...], pick_out[...])
-        sent = sent[0:64] + sent[64:128] + sent[128:192]
-        for tile in range(4):
-            top = sent[0:32, 128 * tile : 128 * tile + 128]
-            bottom = sent[32:64, 128 * tile : 128 * tile + 128]
-            outgoing[turn, 2 * tile] = jnp.where(half, top, pltpu.roll(bottom, 64, 1))
-            outgoing[turn, 2 * tile + 1] = jnp.where(half, pltpu.roll(top, 64, 1), bottom)
-
-    def apply(turn, beside):
-        for index in (0, 2, 5, 7, 1, 6, 3, 4):
-            pltpu.make_async_remote_copy(
-                src_ref=outgoing.at[turn, index],
-                dst_ref=arrived.at[turn, 7 - index],
-                send_sem=halo_send.at[turn],
-                recv_sem=halo_recv.at[turn],
-                device_id=partners[index],
-                device_id_type=MESH,
-            ).start()
-        high, middle, low = split(field[...])
         around[...] = dot(
-            constants[pl.ds(64, 80), pl.ds(0, 192)],
+            constants[pl.ds(0, 80), pl.ds(0, 192)],
             jnp.concatenate([high, middle, low, high, high, middle], axis=0)
         )
+
+        def gradient(axis, component):
+            column = pl.ds(128 * component, 128)
+            return (
+                around[pl.ds(0, 20), column] * geometry[pl.ds(axis, 1), :]
+                + around[pl.ds(24, 20), column] * geometry[pl.ds(3 + axis, 1), :]
+                + around[pl.ds(48, 20), column] * geometry[pl.ds(6 + axis, 1), :]
+            )
+
+        for component in range(3):
+            after, before = (component + 1) % 3, (component + 2) % 3
+            curl_e = gradient(after, before) - gradient(before, after)
+            curl_h = gradient(after, 3 + before) - gradient(before, 3 + after)
+            image[component] = (
+                material[pl.ds(0, 1), :] * curl_h - material[pl.ds(2, 1), :] * vector[component]
+            )
+            image[3 + component] = -material[pl.ds(1, 1), :] * curl_e
         beside()
-        found = dot(parts[...], pick_in[pl.ds(0, 512), :])
+        sources = [table[:, pl.ds(128 * tile, 128)] for tile in range(4)]
+        for face in range(4):
+            lane = pl.ds(128 * face, 128)
+            others[:, lane] = pick(None, sources, index_in[pl.ds(face, 1), :], 0)
         pltpu.make_async_copy(arrived.at[turn], arrived.at[turn], halo_recv.at[turn]).wait()
-        tops = []
-        bottoms = []
+        sources = []
         for tile in range(4):
             even = arrived[turn, 2 * tile]
             odd = arrived[turn, 2 * tile + 1]
-            tops.append(jnp.where(half, even, pltpu.roll(odd, 64, 1)))
-            bottoms.append(jnp.where(half, pltpu.roll(even, 64, 1), odd))
-        far = jnp.concatenate(
-            [jnp.concatenate(tops, axis=1), jnp.concatenate(bottoms, axis=1)], axis=0
+            sources.append(
+                jnp.concatenate(
+                    [
+                        jnp.where(half, even, pltpu.roll(odd, 64, 1)),
+                        jnp.where(half, pltpu.roll(even, 64, 1), odd),
+                    ],
+                    axis=0,
+                )
+            )
+        found = jnp.concatenate(
+            [
+                pick(
+                    others[:, pl.ds(128 * face, 128)], sources, index_in[pl.ds(face, 1), :], 4
+                )
+                for face in range(4)
+            ],
+            axis=1,
         )
-        far = jnp.concatenate(split(far), axis=0)
-        found = found + dot(far, pick_in[pl.ds(512, 512), :])
-        turned = dot(constants[pl.ds(176, 288), pl.ds(0, 192)], found.astype(jnp.bfloat16))
+        rotated[...] = dot(
+            constants[pl.ds(112, 192), pl.ds(0, 192)], jnp.concatenate(split(found), axis=0)
+        )
         for face in range(4):
-            lane = slice(128 * face, 128 * face + 128)
+            lane = pl.ds(128 * face, 128)
             spin = turns[pl.ds(face, 1), :]
             wall = flags[pl.ds(face, 1), :] == 1
             weight = 0.5 * scale[pl.ds(face, 1), :]
             n_x = normals[0, pl.ds(face, 1), :]
             n_y = normals[1, pl.ds(face, 1), :]
             n_z = normals[2, pl.ds(face, 1), :]
-            jumps = []
-            for component in range(6):
-                here = inside[pl.ds(16 * face, 16), pl.ds(128 * component, 128)]
-                other = jnp.where(
-                    spin == 0,
-                    turned[16 * component : 16 * component + 16, lane],
-                    jnp.where(
-                        spin == 1,
-                        turned[96 + 16 * component : 112 + 16 * component, lane],
-                        turned[192 + 16 * component : 208 + 16 * component, lane],
-                    ),
-                )
-                other = jnp.where(wall, -here if component < 3 else here, other)
-                jumps.append(other - here)
-            e_x, e_y, e_z, h_x, h_y, h_z = jumps
-            along_e = n_x * e_x + n_y * e_y + n_z * e_z
-            along_h = n_x * h_x + n_y * h_y + n_z * h_z
-            terms = [
-                n_y * h_z - n_z * h_y + e_x - along_e * n_x,
-                n_z * h_x - n_x * h_z + e_y - along_e * n_y,
-                n_x * h_y - n_y * h_x + e_z - along_e * n_z,
-                n_z * e_y - n_y * e_z + h_x - along_h * n_x,
-                n_x * e_z - n_z * e_x + h_y - along_h * n_y,
-                n_y * e_x - n_x * e_y + h_z - along_h * n_z,
-            ]
-            for component in range(6):
-                flux[pl.ds(16 * face, 16), pl.ds(128 * component, 128)] = (
-                    terms[component] * weight
-                )
+            for first_node, count in ((0, 8), (8, 2)):
+                jumps = []
+                for component in range(6):
+                    row = packed_row(component, first_node)
+                    here = table[pl.ds(row, count), lane]
+                    other = jnp.where(
+                        spin == 0,
+                        rotated[pl.ds(row, count), lane],
+                        jnp.where(
+                            spin == 1,
+                            rotated[pl.ds(64 + row, count), lane],
+                            rotated[pl.ds(128 + row, count), lane],
+                        ),
+                    )
+                    other = jnp.where(wall, -here if component < 3 else here, other)
+                    jumps.append(other - here)
+                e_x, e_y, e_z, h_x, h_y, h_z = jumps
+                along_e = n_x * e_x + n_y * e_y + n_z * e_z
+                along_h = n_x * h_x + n_y * h_y + n_z * h_z
+                terms = [
+                    n_y * h_z - n_z * h_y + e_x - along_e * n_x,
+                    n_z * h_x - n_x * h_z + e_y - along_e * n_y,
+                    n_x * h_y - n_y * h_x + e_z - along_e * n_z,
+                    n_z * e_y - n_y * e_z + h_x - along_h * n_x,
+                    n_x * e_z - n_z * e_x + h_y - along_h * n_y,
+                    n_y * e_x - n_x * e_y + h_z - along_h * n_z,
+                ]
+                for component in range(6):
+                    place = pl.ds(16 * face + first_node, count)
+                    flux[place, pl.ds(128 * component, 128)] = terms[component] * weight
         high, middle, low = split(flux[...])
-        lifted = dot(constants[pl.ds(144, 32), :], jnp.concatenate([high, high, middle, low], axis=0))
-
-        def gradient(axis, component):
-            column = pl.ds(128 * component, 128)
-            return (
-                around[pl.ds(0, 20), column] * geometry[pl.ds(axis, 1), :]
-                + around[pl.ds(24, 20), column] * geometry[pl.ds(3 + axis, 1), :]
-                + around[pl.ds(48, 20), column] * geometry[pl.ds(6 + axis, 1), :]
-            )
-
-        for component in range(3):
-            after, before = (component + 1) % 3, (component + 2) % 3
-            curl_e = gradient(after, before) - gradient(before, after)
-            curl_h = gradient(after, 3 + before) - gradient(before, 3 + after)
+        lifted = dot(constants[pl.ds(80, 32), :], jnp.concatenate([high, high, middle, low], axis=0))
+        for component in range(6):
             raised = lifted[0:20, 128 * component : 128 * component + 128]
-            image[component] = (
-                material[pl.ds(0, 1), :] * (curl_h + raised)
-                - material[pl.ds(2, 1), :] * vector[component]
-            )
-            raised = lifted[0:20, 384 + 128 * component : 512 + 128 * component]
-            image[3 + component] = material[pl.ds(1, 1), :] * (raised - curl_e)
+            image[component] += material[pl.ds(component // 3, 1), :] * raised
 
     sub8 = iota((8, 128), 0)
     sub24 = iota((24, 128), 0)
@@ -439,21 +441,19 @@
     eye = sub24 == lane24
 
     def inner(vector_ref, *pairs):
-        def some(step, held):
+        def some(component, held):
             held = list(held)
-            for inner_step in range(4):
-                node = 4 * step + inner_step
-                for component in range(6):
-                    held[component % 3] += (
-                        stored[component, node] * vector_ref[component, pl.ds(node, 1), :]
-                    )
+            for node in range(20):
+                held[node % 3] += (
+                    stored[component, node] * vector_ref[component, pl.ds(node, 1), :]
+                )
             return tuple(held)
 
         zero = jnp.zeros((kept, 128), jnp.float32)
         for place, (left, right) in enumerate(pairs):
             partial = jnp.sum(left[...] * right[...], axis=0)
             work[pl.ds(kept + place, 1), :] = jnp.sum(partial, axis=0, keepdims=True)
-        one, two, three = lax.fori_loop(0, 5, some, (zero, zero, zero))
+        one, two, three = lax.fori_loop(0, 6, some, (zero, zero, zero))
         work[pl.ds(0, kept), :] = one + two + three
         return to_row(jnp.sum(work[...], axis=1, keepdims=True))
 
@@ -551,31 +551,36 @@
 
     field[pl.ds(16, 16), :] = jnp.zeros((16, 768), jnp.float32)
     table[pl.ds(56, 8), :] = jnp.zeros((8, 512), jnp.float32)
+    flux[...] = jnp.zeros((64, 768), jnp.float32)
     held_bound[...] = jnp.ones((1, 128), jnp.float32)
     side_row[...] = jnp.zeros((1, 128), jnp.float32)
     work[...] = jnp.zeros((24, 128), jnp.float32)
     hessenberg[...] = jnp.zeros((2, kept + 2), jnp.float32)
     loads[1].wait()
-    loads[2].wait()
-    for load in loads[3:]:
+    for load in loads[2:]:
         load.start()
-    constants[pl.ds(0, 64), :] = constants_wide[pl.ds(0, 64), :].astype(jnp.bfloat16)
     for component in range(6):
         vector[component] = stored[component, :, kept - 1, :]
-    prepare(0)
-    for load in loads[3:]:
-        load.wait()
-    constants[pl.ds(64, 400), :] = constants_wide[pl.ds(64, 400), :].astype(jnp.bfloat16)
-    pl.semaphore_wait(barrier, len(greeted))
 
     def step(turn, carry):
         first_step = turn == 0
         sums = sums_b.at[turn]
 
+        def ready():
+            @pl.when(first_step)
+            def _():
+                for load in loads[2:]:
+                    load.wait()
+                constants[...] = constants_wide[...].astype(jnp.bfloat16)
+
         def beside():
             @pl.when(first_step)
             def _():
-                fill_pick_in()
+                for face in range(4):
+                    named = source[pl.ds(face, 1), :]
+                    index_in[pl.ds(face, 1), :] = jnp.where(
+                        named >= 512 + 4 * 64, named - 64, named
+                    )
                 fill_gram()
                 packed = (
                     gram[pl.ds(0, 8), :]
@@ -588,7 +593,13 @@
             def _():
                 side_row[...] = pltpu.roll(inner(vector, (vector, vector)), 32, 1)
 
-        apply(turn, beside)
+        def greeting():
+            @pl.when(first_step)
+            def _():
+                pl.semaphore_wait(barrier, len(greeted))
+
+        prepare(turn, greeting)
+        apply(turn, ready, beside)
 
         row = inner(image, (vector, image), (image, image))
         begin(row + side_row[...], sums, narrow, turn, 0)
@@ -653,11 +664,6 @@
         hessenberg[pl.ds(turn, 1), :] = jnp.where(
             lane1 == kept + 1, jnp.where(first_step, 0.0, height), column_row
         )[:, 0:24]
-
-        @pl.when(first_step)
-        def _():
-            prepare(1)
-
         return carry
 
     lax.fori_loop(0, 2, step, 0)
@@ -690,7 +696,7 @@
     anywhere = pl.BlockSpec(memory_space=pl.ANY)
     vmem = pl.BlockSpec(memory_space=pltpu.VMEM)
     return pl.pallas_call(
-        functools.partial(kernel, (n_gx, n_gy, total)),
+        functools.partial(kernel, (n_gx, n_gy, total, element_tables()[2])),
         out_shape=(
             pltpu.VMEM((2, components, nodes, local_count), f32),
             pltpu.VMEM((2, kept + 2), f32),
@@ -707,18 +713,18 @@
             pltpu.VMEM(neighbour_source.shape, jnp.int32),
             pltpu.VMEM(node_rotation.shape, jnp.int32),
             pltpu.VMEM(boundary_flag.shape, jnp.int32),
-            pltpu.VMEM((464, 256), f32),
-            pltpu.VMEM((464, 256), bf16),
+            pltpu.VMEM((304, 256), f32),
+            pltpu.VMEM((304, 256), bf16),
             pltpu.VMEM((components, nodes, local_count), f32),
             pltpu.VMEM((32, 768), f32),
-            pltpu.VMEM((64, 768), f32),
             pltpu.VMEM((80, 768), f32),
             pltpu.VMEM((64, 512), f32),
-            pltpu.VMEM((192, 512), bf16),
+            pltpu.VMEM((64, 512), f32),
+            pltpu.VMEM((192, 512), f32),
             pltpu.VMEM((components, nodes, local_count), f32),
             pltpu.VMEM((64, 768), f32),
-            pltpu.VMEM((512, 512), bf16),
-            pltpu.VMEM((1024, 512), bf16),
+            pltpu.VMEM((4, 128), jnp.int32),
+            pltpu.VMEM((4, 128), jnp.int32),
             pltpu.VMEM((24, 128), f32),
             pltpu.VMEM((1, 128), f32),
             pltpu.VMEM((1, 128), f32),

time: 51.4 us -> 51.3 us (level)
  no operation moved by 1% of the time
where the time goes in v4:
time: 51.3 us; the launch traced here: 51.1 us
  Pallas kernels  49.2 us (96%)
  local copies, waits for them, and re-layouts  1.27 us (2%)
  between operations  0.64 us (1%)
    pallas_call x1, Pallas kernels, body(): pl.pallas_call(functools.partial(kernel, (n_gx, n_gy, total, element_tabl...  49.2 us

profile of v4, /device:TPU:1, one launch (start us, length us, event | category | flops | bytes accessed | tf_op | source)
XLA Modules:
  0.0 51.1 jit_solution(7666340158832654419)
XLA Ops:
  0.6 49.2 %shard_map.113 = (f32[2,6,20,128]{3,2,1,0:T(8,128)S(1)}, f32[2,24]{1,0:T(2,128)S(1)}) custom-call(f32[6,20,22,128]{3,2,1,0:T(8,128)} %bitcast.1, f32[9,128]{1,0:T(8,128)} %geometry_hbm.1, f32[3,4,128]{2,1,0:T(4,128)} %normals_hbm.1, f32[4,128]{1,0:T(4,128)} %scale_hbm.1, f32[3,128]{1,0:T(4,128)} %material_hbm.1, s32[3,3,64]{2,1,0:T(4,128)} %send_list_hbm.1, ...), custom_call_target="tpu_custom_call" | custom-call | tf_op jit(solution)/shard_map/pallas_call | solution.py:698
  49.9 0.7 %copy.12 = f32[2,6,20,128]{3,0,2,1:T(2,128)} copy(f32[2,6,20,128]{3,2,1,0:T(8,128)S(1)} %get-tuple-element.2) | data formatting | bytes 245760 | tf_op jit(solution)/shard_map/pallas_call | solution.py:698
  50.6 0.6 %copy.14 = f32[2,24]{1,0:T(2,128)} copy(f32[2,24]{1,0:T(2,128)S(1)} %get-tuple-element.5) | data formatting | bytes 384

commit v5 on v4

--- a/solution.py
+++ b/solution.py
@@ -10,7 +10,6 @@
 from jax.sharding import PartitionSpec as P
 
 MESH = pl.DeviceIdType.MESH
-X_CHIPS = 4
 OPERANDS = (0, 80, 112)
 DIRECTIONS = (0, 1, 2, 3, 5, 6, 7, 8)
 
@@ -257,27 +256,13 @@
                 turned_on(gy, (direction % 3 - 1) % n_gy, n_gy),
             )
         )
-    across = lax.rem(gx, X_CHIPS)
-    up = lax.div(gx, X_CHIPS)
-    rows_up = n_gx // X_CHIPS
 
     def farthest_first(size):
         return sorted(range(1, size), key=lambda step: -min(step, size - step))
 
     on_gy = (n_gy, gy, [(gx, turned_on(gy, step, n_gy)) for step in farthest_first(n_gy)])
     on_gx = (n_gx, gx, [(turned_on(gx, step, n_gx), gy) for step in farthest_first(n_gx)])
-    on_y = (
-        rows_up,
-        up,
-        [(turned_on(gx, X_CHIPS * step, n_gx), gy) for step in farthest_first(rows_up)],
-    )
-    on_x = (
-        X_CHIPS,
-        across,
-        [(gx - across + turned_on(across, step, X_CHIPS), gy) for step in range(1, X_CHIPS)],
-    )
-    narrow = (on_gy, on_gx)
-    broad = (on_y, on_gy, on_x)
+    groups = (on_gy, on_gx)
 
     barrier = pltpu.get_barrier_semaphore()
     greeted = list(partners)
@@ -507,7 +492,7 @@
                 old = gram[pl.ds(first, count), :]
                 gram[pl.ds(first, count), :] = jnp.where(lane >= first, held, old)
 
-    def begin(value, buffer, groups, which, stage):
+    def begin(value, buffer, which, stage):
         size, mine, peers = groups[stage]
         buffer[stage, mine] = value
         for peer in peers:
@@ -520,7 +505,7 @@
                 device_id_type=MESH,
             ).start()
 
-    def finish(buffer, groups, which, stage):
+    def finish(buffer, which, stage):
         size, mine, peers = groups[stage]
         if size > 1:
             others = buffer.at[stage, pl.ds(0, size - 1)]
@@ -587,7 +572,7 @@
                     + pltpu.roll(gram[pl.ds(8, 8), :], 32, 1)
                     + pltpu.roll(gram[pl.ds(16, 8), :], 64, 1)
                 )
-                begin(packed, sums_a, broad, 2, 0)
+                begin(packed, sums_a, 2, 0)
 
             @pl.when(jnp.logical_not(first_step))
             def _():
@@ -602,18 +587,17 @@
         apply(turn, ready, beside)
 
         row = inner(image, (vector, image), (image, image))
-        begin(row + side_row[...], sums, narrow, turn, 0)
+        begin(row + side_row[...], sums, turn, 0)
 
         @pl.when(first_step)
         def _():
-            begin(finish(sums_a, broad, 2, 0), sums_a, broad, 2, 1)
-
-        begin(finish(sums, narrow, turn, 0), sums, narrow, turn, 1)
+            begin(finish(sums_a, 2, 0), sums_a, 2, 1)
+
+        begin(finish(sums, turn, 0), sums, turn, 1)
 
         @pl.when(first_step)
         def _():
-            begin(finish(sums_a, broad, 2, 1), sums_a, broad, 2, 2)
-            packed = finish(sums_a, broad, 2, 2) * (1.0 / total)
+            packed = finish(sums_a, 2, 1) * (1.0 / total)
             products = jnp.concatenate(
                 [packed, pltpu.roll(packed, 96, 1), pltpu.roll(packed, 64, 1)], axis=0
             )
@@ -621,7 +605,7 @@
 
         products = gram[...]
         own = jnp.sum(jnp.where(eye, products, 0.0), axis=1, keepdims=True)
-        message = finish(sums, narrow, turn, 1) * (1.0 / total)
+        message = finish(sums, turn, 1) * (1.0 / total)
 
         bound = held_bound[...][:, 0:1]
         row = jnp.where(lane1 < kept + turn, message, 0.0)
@@ -670,7 +654,7 @@
     for turn in range(2):
         pltpu.make_async_copy(outgoing.at[turn], outgoing.at[turn], halo_send.at[turn]).wait()
     for which in range(3):
-        for stage, (size, _, _) in enumerate(broad if which == 2 else narrow):
+        for stage, (size, _, _) in enumerate(groups):
             if size > 1:
                 buffer = sums_a if which == 2 else sums_b.at[which]
                 others = buffer.at[stage, pl.ds(0, size - 1)]
@@ -733,7 +717,7 @@
             pltpu.VMEM((components, nodes, local_count), f32),
             pltpu.VMEM((2, 8, 32, 128), f32),
             pltpu.VMEM((2, 8, 32, 128), f32),
-            pltpu.VMEM((3, max(n_gx // X_CHIPS, n_gy, X_CHIPS), 8, 128), f32),
+            pltpu.VMEM((2, max(n_gx, n_gy), 8, 128), f32),
             pltpu.VMEM((2, 2, max(n_gx, n_gy), 1, 128), f32),
             pltpu.SemaphoreType.DMA((12,)),
             pltpu.SemaphoreType.DMA((2,)),

time: 51.3 us -> 51.5 us (level)
  no operation moved by 1% of the time
where the time goes in v5:
time: 51.5 us; the launch traced here: 51.3 us
  Pallas kernels  49.4 us (96%)
  local copies, waits for them, and re-layouts  1.27 us (2%)
  between operations  0.64 us (1%)
    pallas_call x1, Pallas kernels, body(): pl.pallas_call(functools.partial(kernel, (n_gx, n_gy, total, element_tabl...  49.4 us

profile of v5, /device:TPU:1, one launch (start us, length us, event | category | flops | bytes accessed | tf_op | source)
XLA Modules:
  0.0 51.3 jit_solution(5758379244876880221)
XLA Ops:
  0.6 49.4 %shard_map.113 = (f32[2,6,20,128]{3,2,1,0:T(8,128)S(1)}, f32[2,24]{1,0:T(2,128)S(1)}) custom-call(f32[6,20,22,128]{3,2,1,0:T(8,128)} %bitcast.1, f32[9,128]{1,0:T(8,128)} %geometry_hbm.1, f32[3,4,128]{2,1,0:T(4,128)} %normals_hbm.1, f32[4,128]{1,0:T(4,128)} %scale_hbm.1, f32[3,128]{1,0:T(4,128)} %material_hbm.1, s32[3,3,64]{2,1,0:T(4,128)} %send_list_hbm.1, ...), custom_call_target="tpu_custom_call" | custom-call | tf_op jit(solution)/shard_map/pallas_call | solution.py:682
  50.1 0.7 %copy.12 = f32[2,6,20,128]{3,0,2,1:T(2,128)} copy(f32[2,6,20,128]{3,2,1,0:T(8,128)S(1)} %get-tuple-element.2) | data formatting | bytes 245760 | tf_op jit(solution)/shard_map/pallas_call | solution.py:682
  50.8 0.6 %copy.14 = f32[2,24]{1,0:T(2,128)} copy(f32[2,24]{1,0:T(2,128)S(1)} %get-tuple-element.5) | data formatting | bytes 384

commit v6 on v5

--- a/solution.py
+++ b/solution.py
@@ -10,6 +10,8 @@
 from jax.sharding import PartitionSpec as P
 
 MESH = pl.DeviceIdType.MESH
+X_CHIPS = 4
+CORES = 2
 OPERANDS = (0, 80, 112)
 DIRECTIONS = (0, 1, 2, 3, 5, 6, 7, 8)
 
@@ -257,17 +259,52 @@
             )
         )
 
-    def farthest_first(size):
-        return sorted(range(1, size), key=lambda step: -min(step, size - step))
-
-    on_gy = (n_gy, gy, [(gx, turned_on(gy, step, n_gy)) for step in farthest_first(n_gy)])
-    on_gx = (n_gx, gx, [(turned_on(gx, step, n_gx), gy) for step in farthest_first(n_gx)])
-    groups = (on_gy, on_gx)
+    across = lax.rem(gx, X_CHIPS)
+    up = lax.div(gx, X_CHIPS)
+    core = lax.rem(gy, CORES)
+    along = lax.div(gy, CORES)
+    odd = lax.rem(across, 2)
+    rows_up = n_gx // X_CHIPS
+    layers = n_gy // CORES
+    beside_x = gx + 1 - 2 * odd
+    facing_x = gx + X_CHIPS - 1 - 2 * across
+    hops_first = []
+    for step in range(layers):
+        for other in range(2):
+            hops_first.append((min(step, layers - step) + other, step, other))
+    hops_second = []
+    for step in range(rows_up):
+        for other in range(2):
+            for flip in range(CORES):
+                hops_second.append((min(step, rows_up - step) + other + flip / 2, step, other, flip))
+    first_peers = [
+        (hops, (beside_x if other else gx, turned_on(gy, CORES * step, n_gy)))
+        for hops, step, other in sorted(hops_first, reverse=True)
+        if hops > 0
+    ]
+    second_peers = [
+        (
+            hops,
+            (
+                turned_on(facing_x if other else gx, X_CHIPS * step, n_gx),
+                turned_on(core, flip, CORES) + gy - core,
+            ),
+        )
+        for hops, step, other, flip in sorted(hops_second, reverse=True)
+        if hops > 0
+    ]
+    groups = (
+        (2 * layers, 2 * along + odd, [peer for _, peer in first_peers]),
+        (
+            2 * CORES * rows_up,
+            (lax.div(across, 2) * rows_up + up) * CORES + core,
+            [peer for _, peer in second_peers],
+        ),
+    )
 
     barrier = pltpu.get_barrier_semaphore()
-    greeted = list(partners)
-    greeted += [(gx, turned_on(gy, step, n_gy)) for step in range(2, n_gy - 1)]
-    greeted += [(turned_on(gx, step, n_gx), gy) for step in range(2, n_gx - 1)]
+    greeted = sorted(first_peers + second_peers, key=lambda entry: -entry[0])
+    greeted = [peer for _, peer in greeted] + partners
     for peer in greeted:
         pl.semaphore_signal(barrier, inc=1, device_id=peer, device_id_type=MESH)
 
@@ -677,6 +714,7 @@
     kept, components, nodes, local_count = basis.shape
     total = float(components * nodes * local_count * n_gx * n_gy)
     f32, bf16 = jnp.float32, jnp.bfloat16
+    members = max(2 * n_gy // CORES, 2 * CORES * n_gx // X_CHIPS)
     anywhere = pl.BlockSpec(memory_space=pl.ANY)
     vmem = pl.BlockSpec(memory_space=pltpu.VMEM)
     return pl.pallas_call(
@@ -717,8 +755,8 @@
             pltpu.VMEM((components, nodes, local_count), f32),
             pltpu.VMEM((2, 8, 32, 128), f32),
             pltpu.VMEM((2, 8, 32, 128), f32),
-            pltpu.VMEM((2, max(n_gx, n_gy), 8, 128), f32),
-            pltpu.VMEM((2, 2, max(n_gx, n_gy), 1, 128), f32),
+            pltpu.VMEM((2, members, 8, 128), f32),
+            pltpu.VMEM((2, 2, members, 1, 128), f32),
             pltpu.SemaphoreType.DMA((12,)),
             pltpu.SemaphoreType.DMA((2,)),
             pltpu.SemaphoreType.DMA((2,)),

time: 51.5 us -> 51.9 us (level)
  no operation moved by 1% of the time
where the time goes in v6:
time: 51.9 us; the launch traced here: 51.7 us
  Pallas kernels  49.8 us (96%)
  local copies, waits for them, and re-layouts  1.27 us (2%)
  between operations  0.64 us (1%)
    pallas_call x1, Pallas kernels, body(): pl.pallas_call(functools.partial(kernel, (n_gx, n_gy, total, element_tabl...  49.8 us

profile of v6, /device:TPU:1, one launch (start us, length us, event | category | flops | bytes accessed | tf_op | source)
XLA Modules:
  0.0 51.7 jit_solution(1195414254458170516)
XLA Ops:
  0.6 49.8 %shard_map.113 = (f32[2,6,20,128]{3,2,1,0:T(8,128)S(1)}, f32[2,24]{1,0:T(2,128)S(1)}) custom-call(f32[6,20,22,128]{3,2,1,0:T(8,128)} %bitcast.1, f32[9,128]{1,0:T(8,128)} %geometry_hbm.1, f32[3,4,128]{2,1,0:T(4,128)} %normals_hbm.1, f32[4,128]{1,0:T(4,128)} %scale_hbm.1, f32[3,128]{1,0:T(4,128)} %material_hbm.1, s32[3,3,64]{2,1,0:T(4,128)} %send_list_hbm.1, ...), custom_call_target="tpu_custom_call" | custom-call | tf_op jit(solution)/shard_map/pallas_call | solution.py:720
  50.5 0.7 %copy.12 = f32[2,6,20,128]{3,0,2,1:T(2,128)} copy(f32[2,6,20,128]{3,2,1,0:T(8,128)S(1)} %get-tuple-element.2) | data formatting | bytes 245760 | tf_op jit(solution)/shard_map/pallas_call | solution.py:720
  51.2 0.6 %copy.14 = f32[2,24]{1,0:T(2,128)} copy(f32[2,24]{1,0:T(2,128)S(1)} %get-tuple-element.5) | data formatting | bytes 384

commit v7 on v6

--- a/solution.py
+++ b/solution.py
@@ -271,36 +271,42 @@
     hops_first = []
     for step in range(layers):
         for other in range(2):
-            hops_first.append((min(step, layers - step) + other, step, other))
+            for flip in range(CORES):
+                hops_first.append((min(step, layers - step) + other + flip / 2, step, other, flip))
     hops_second = []
     for step in range(rows_up):
         for other in range(2):
-            for flip in range(CORES):
-                hops_second.append((min(step, rows_up - step) + other + flip / 2, step, other, flip))
+            hops_second.append((min(step, rows_up - step) + other, step, other))
     first_peers = [
-        (hops, (beside_x if other else gx, turned_on(gy, CORES * step, n_gy)))
-        for hops, step, other in sorted(hops_first, reverse=True)
+        (
+            hops,
+            (
+                beside_x if other else gx,
+                turned_on(gy, CORES * step, n_gy) - core + turned_on(core, flip, CORES),
+            ),
+        )
+        for hops, step, other, flip in sorted(hops_first, reverse=True)
         if hops > 0
     ]
     second_peers = [
-        (
-            hops,
-            (
-                turned_on(facing_x if other else gx, X_CHIPS * step, n_gx),
-                turned_on(core, flip, CORES) + gy - core,
-            ),
-        )
-        for hops, step, other, flip in sorted(hops_second, reverse=True)
+        (hops, (turned_on(facing_x if other else gx, X_CHIPS * step, n_gx), gy))
+        for hops, step, other in sorted(hops_second, reverse=True)
         if hops > 0
     ]
-    groups = (
-        (2 * layers, 2 * along + odd, [peer for _, peer in first_peers]),
-        (
-            2 * CORES * rows_up,
-            (lax.div(across, 2) * rows_up + up) * CORES + core,
-            [peer for _, peer in second_peers],
-        ),
+    first_group = (
+        2 * CORES * layers,
+        (2 * along + odd) * CORES + core,
+        [peer for _, peer in first_peers],
     )
+    second_group = (
+        2 * rows_up,
+        lax.div(across, 2) * rows_up + up,
+        [peer for _, peer in second_peers],
+    )
+
+    def group_of(which, stage):
+        is_gram = isinstance(which, int) and which == 2
+        return second_group if (stage == 1) != is_gram else first_group
 
     barrier = pltpu.get_barrier_semaphore()
     greeted = sorted(first_peers + second_peers, key=lambda entry: -entry[0])
@@ -530,7 +536,7 @@
                 gram[pl.ds(first, count), :] = jnp.where(lane >= first, held, old)
 
     def begin(value, buffer, which, stage):
-        size, mine, peers = groups[stage]
+        size, mine, peers = group_of(which, stage)
         buffer[stage, mine] = value
         for peer in peers:
             pltpu.make_async_remote_copy(
@@ -543,7 +549,7 @@
             ).start()
 
     def finish(buffer, which, stage):
-        size, mine, peers = groups[stage]
+        size, mine, peers = group_of(which, stage)
         if size > 1:
             others = buffer.at[stage, pl.ds(0, size - 1)]
             pltpu.make_async_copy(others, others, sum_recv.at[which, stage]).wait()
@@ -691,7 +697,8 @@
     for turn in range(2):
         pltpu.make_async_copy(outgoing.at[turn], outgoing.at[turn], halo_send.at[turn]).wait()
     for which in range(3):
-        for stage, (size, _, _) in enumerate(groups):
+        for stage in range(2):
+            size = group_of(which, stage)[0]
             if size > 1:
                 buffer = sums_a if which == 2 else sums_b.at[which]
                 others = buffer.at[stage, pl.ds(0, size - 1)]
@@ -714,7 +721,7 @@
     kept, components, nodes, local_count = basis.shape
     total = float(components * nodes * local_count * n_gx * n_gy)
     f32, bf16 = jnp.float32, jnp.bfloat16
-    members = max(2 * n_gy // CORES, 2 * CORES * n_gx // X_CHIPS)
+    members = max(2 * n_gy, 2 * n_gx // X_CHIPS)
     anywhere = pl.BlockSpec(memory_space=pl.ANY)
     vmem = pl.BlockSpec(memory_space=pltpu.VMEM)
     return pl.pallas_call(

time: 51.9 us -> 50.6 us (0.975)
  Pallas kernels: 49.8 us -> 48.6 us
    pallas_call x1, Pallas kernels: 49.8 us -> 48.6 us  [body(): pl.pallas_call(functools.partial(kernel, (n_gx, n_gy, total, element_tabl...]
where the time goes in v7:
time: 50.6 us; the launch traced here: 50.5 us
  Pallas kernels  48.6 us (96%)
  local copies, waits for them, and re-layouts  1.27 us (3%)
  between operations  0.64 us (1%)
    pallas_call x1, Pallas kernels, body(): pl.pallas_call(functools.partial(kernel, (n_gx, n_gy, total, element_tabl...  48.6 us

profile of v7, /device:TPU:1, one launch (start us, length us, event | category | flops | bytes accessed | tf_op | source)
XLA Modules:
  0.0 50.5 jit_solution(16593112497502144180)
XLA Ops:
  0.6 48.6 %shard_map.113 = (f32[2,6,20,128]{3,2,1,0:T(8,128)S(1)}, f32[2,24]{1,0:T(2,128)S(1)}) custom-call(f32[6,20,22,128]{3,2,1,0:T(8,128)} %bitcast.1, f32[9,128]{1,0:T(8,128)} %geometry_hbm.1, f32[3,4,128]{2,1,0:T(4,128)} %normals_hbm.1, f32[4,128]{1,0:T(4,128)} %scale_hbm.1, f32[3,128]{1,0:T(4,128)} %material_hbm.1, s32[3,3,64]{2,1,0:T(4,128)} %send_list_hbm.1, ...), custom_call_target="tpu_custom_call" | custom-call | tf_op jit(solution)/shard_map/pallas_call | solution.py:727
  49.2 0.7 %copy.12 = f32[2,6,20,128]{3,0,2,1:T(2,128)} copy(f32[2,6,20,128]{3,2,1,0:T(8,128)S(1)} %get-tuple-element.2) | data formatting | bytes 245760 | tf_op jit(solution)/shard_map/pallas_call | solution.py:727
  49.9 0.6 %copy.14 = f32[2,24]{1,0:T(2,128)} copy(f32[2,24]{1,0:T(2,128)S(1)} %get-tuple-element.5) | data formatting | bytes 384

commit v8 on v7

--- a/solution.py
+++ b/solution.py
@@ -343,7 +343,6 @@
                     table[row, pl.ds(128 * face, 128)] = vector[
                         component, pl.ds(int(face_nodes[node, face]), 1), :
                     ]
-        greeting()
         sources = [table[:, pl.ds(128 * tile, 128)] for tile in range(4)]
         for tile in (0, 3, 1, 2):
             sent = pick(None, sources, index_out[pl.ds(tile, 1), :], 0)
@@ -351,15 +350,16 @@
             bottom = sent[32:64]
             outgoing[turn, 2 * tile] = jnp.where(half, top, pltpu.roll(bottom, 64, 1))
             outgoing[turn, 2 * tile + 1] = jnp.where(half, pltpu.roll(top, 64, 1), bottom)
-            for index in (2 * tile, 2 * tile + 1):
-                pltpu.make_async_remote_copy(
-                    src_ref=outgoing.at[turn, index],
-                    dst_ref=arrived.at[turn, 7 - index],
-                    send_sem=halo_send.at[turn],
-                    recv_sem=halo_recv.at[turn],
-                    device_id=partners[index],
-                    device_id_type=MESH,
-                ).start()
+        greeting()
+        for index in (0, 1, 6, 7, 2, 5, 3, 4):
+            pltpu.make_async_remote_copy(
+                src_ref=outgoing.at[turn, index],
+                dst_ref=arrived.at[turn, 7 - index],
+                send_sem=halo_send.at[turn],
+                recv_sem=halo_recv.at[turn],
+                device_id=partners[index],
+                device_id_type=MESH,
+            ).start()
 
     def apply(turn, ready, beside):
         ready()

time: 50.6 us -> 50.6 us (level)
  no operation moved by 1% of the time
where the time goes in v8:
time: 50.6 us; the launch traced here: 50.5 us
  Pallas kernels  48.5 us (96%)
  local copies, waits for them, and re-layouts  1.27 us (3%)
  between operations  0.64 us (1%)
    pallas_call x1, Pallas kernels, body(): pl.pallas_call(functools.partial(kernel, (n_gx, n_gy, total, element_tabl...  48.5 us

profile of v8, /device:TPU:1, one launch (start us, length us, event | category | flops | bytes accessed | tf_op | source)
XLA Modules:
  0.0 50.5 jit_solution(10634805103611844005)
XLA Ops:
  0.6 48.5 %shard_map.113 = (f32[2,6,20,128]{3,2,1,0:T(8,128)S(1)}, f32[2,24]{1,0:T(2,128)S(1)}) custom-call(f32[6,20,22,128]{3,2,1,0:T(8,128)} %bitcast.1, f32[9,128]{1,0:T(8,128)} %geometry_hbm.1, f32[3,4,128]{2,1,0:T(4,128)} %normals_hbm.1, f32[4,128]{1,0:T(4,128)} %scale_hbm.1, f32[3,128]{1,0:T(4,128)} %material_hbm.1, s32[3,3,64]{2,1,0:T(4,128)} %send_list_hbm.1, ...), custom_call_target="tpu_custom_call" | custom-call | tf_op jit(solution)/shard_map/pallas_call | solution.py:727
  49.2 0.7 %copy.12 = f32[2,6,20,128]{3,0,2,1:T(2,128)} copy(f32[2,6,20,128]{3,2,1,0:T(8,128)S(1)} %get-tuple-element.2) | data formatting | bytes 245760 | tf_op jit(solution)/shard_map/pallas_call | solution.py:727
  49.9 0.6 %copy.14 = f32[2,24]{1,0:T(2,128)} copy(f32[2,24]{1,0:T(2,128)S(1)} %get-tuple-element.5) | data formatting | bytes 384
